TPU v7x, 256 devices: a whole 4x4x8 slice. The times are simulated.
256 devices in a mesh: node: 32 (over x, y, core), outer: 8 (over z).
Axes of the slice: x: 4, y: 4, z: 8, core: 2. Of those that a mesh axis runs over, the one named last changes fastest.
Arguments:
- acts: bfloat16 [81920, 14336], P(('node', 'outer')), may hold values from -6 to 6
- cotangent: bfloat16 [81920, 128], P(('node', 'outer')), may hold values from -24 to 24
- signs: int32 [56, 256], replicated, may hold values from -1 to 1, as said below
Outputs:
- rotated_mean: float32 [7168, 256], P(('node', 'outer'))
- grad_mean: bfloat16 [7168, 256], replicated
Inputs may be any that keep to these rules, and one draw needn't show every extreme that they name: `signs`: every entry is -1 or 1.
All inputs are finite; a program needn't handle non-finite values.
Results may differ from a plain program's by a relative error of at most 0.012.
Values may be sent and summed in bfloat16 or wider, within the bound.
No kernel may reach another device: no remote copies, remote signals or barrier semaphores. Data moves between devices by JAX's collectives and lax.ppermute only.
A program may use at most 128 MiB of HBM per device.

v0:
```python
import math

import jax
import jax.numpy as jnp
from jax import lax
from jax.sharding import PartitionSpec as P

COLS = 128
BLK = 256
LEVELS = 15
BLOCKS = 56


def hadamard(size):
    index = jnp.arange(size, dtype=jnp.int32)
    parity = jnp.zeros((size, size), jnp.int32)
    bit = 1
    while bit < size:
        parity = parity + index[:, None] // bit % 2 * (index[None, :] // bit % 2)
        bit = bit * 2
    return jnp.where(parity % 2 == 0, 1.0, -1.0).astype(jnp.float32)


def rotate(partial_value, signs):
    blocks = partial_value.reshape(BLOCKS, BLK, COLS) * signs.astype(jnp.float32)[:, :, None]
    turned = jnp.einsum("ij,bjc->bci", hadamard(BLK), blocks, precision=lax.Precision.HIGHEST)
    return (turned * (1.0 / math.sqrt(BLK))).reshape(BLOCKS * COLS, BLK)


def row_signs(signs, first_row, count):
    row_ids = first_row + jnp.arange(count, dtype=jnp.int32)
    onehot = (row_ids[:, None] // COLS == jnp.arange(BLOCKS, dtype=jnp.int32)[None, :]).astype(
        jnp.float32
    )
    return jnp.dot(onehot, signs.astype(jnp.float32), precision=lax.Precision.HIGHEST)


def unrotate(values, signs, first_row):
    back = jnp.dot(values, hadamard(BLK), precision=lax.Precision.HIGHEST)
    signed = back * row_signs(signs, first_row, values.shape[0])
    return (signed * (1.0 / math.sqrt(BLK))).astype(jnp.bfloat16)


def body(acts, cotangent, signs):
    n_node = lax.axis_size("node")
    n_outer = lax.axis_size("outer")
    devices = n_node * n_outer
    own_rows = BLOCKS * COLS // devices
    partial_value = lax.dot_general(
        acts, cotangent, (((0,), (0,)), ((), ())), preferred_element_type=jnp.float32
    )
    turned = rotate(partial_value, signs)
    largest = lax.pmax(jnp.max(jnp.abs(turned), axis=1), ("node", "outer"))
    scale = largest + 1e-06
    quant = jnp.floor(turned / scale[:, None] * LEVELS + 0.5)
    grouped = lax.psum_scatter(quant.astype(jnp.bfloat16), "node", scatter_dimension=0, tiled=True)
    total = lax.psum_scatter(grouped, "outer", scatter_dimension=0, tiled=True).astype(jnp.float32)
    first_row = lax.axis_index(("node", "outer")) * own_rows
    own_scale = lax.dynamic_slice_in_dim(scale, first_row, own_rows, 0)
    rotated_mean = total * own_scale[:, None] / (LEVELS * devices)
    own_grad = unrotate(rotated_mean, signs, first_row)
    grad_mean = lax.all_gather(own_grad, ("node", "outer"), axis=0, tiled=True)
    return (rotated_mean, grad_mean)


def solution(mesh):
    in_specs = (P(("node", "outer"), None), P(("node", "outer"), None), P())
    out_specs = (P(("node", "outer"), None), P())
    return jax.shard_map(body, mesh=mesh, in_specs=in_specs, out_specs=out_specs, check_vma=False)
```

profile of v0, /device:TPU:33, one launch (start us, length us, event | category | flops | bytes accessed | tf_op | source)
XLA Modules:
  0.0 361.5 jit_solution(10775705310677271601)
XLA Ops:
  7.2 0.0 copy-start
  7.2 0.0 reduce-scatter.4.cloned.1.call-start
  7.3 0.8 copy-done
  8.1 9.8 %fusion.38 = f32[14336,128]{1,0:T(8,128)} fusion(bf16[320,14336]{1,0:T(8,128)(2,1)} %param.3, bf16[320,128]{1,0:T(8,128)(2,1)S(1)} %copy-done), kind=kOutput, calls=%fused_computation.92 | convolution fusion | flops 1174405120 | bytes 16596992 | tf_op jit(solution)/shard_map/dot_general | solution.py:49
  17.8 8.4 %copy.7 = f32[56,256,128]{1,2,0:T(8,128)} copy(f32[56,256,128]{2,1,0:T(8,128)} %bitcast.25) | data formatting | bytes 14680064 | tf_op jit(solution)/shard_map/reshape | solution.py:25
  26.3 10.7 %abs_reduce_fusion = (f32[56,128]{1,0:T(8,128)S(1)}, f32[56,128,256]{2,1,0:T(8,128)}) fusion(s32[256]{0:T(256)S(1)} %get-tuple-element.4, s32[256]{0:T(256)S(1)} %get-tuple-element.5, s32[256]{0:T(256)S(1)} %get-tuple-element.6, s32[256]{0:T(256)S(1)} %get-tuple-element.7, s32[256]{0:T(256)S(1)} %get-tuple-element.8, s32[256]{0:T(256)S(1)} %get-tuple-element.9, ...), kind=kOutput, calls=%fused_computation.4 | convolution fusion | flops 5646312448 | bytes 14774272 | tf_op jit(solution)/shard_map/ij,bjc->bci/dot_general | solution.py:26
  37.0 79.8 %pmax.7 = f32[7168]{0:T(1024)S(1)} all-reduce(f32[7168]{0:T(1024)S(1)} %bitcast.26), channel_id=1, replica_groups=mesh['node'=32,'outer'=8] {'node','outer'}, use_global_device_ids=true, to_apply=%region_1.2 | all-reduce | flops 7168 | bytes 57344 | tf_op jit(solution)/shard_map/pmax | solution.py:53
  116.8 6.3 %fusion.6 = bf16[7168,256]{1,0:T(8,128)(2,1)} fusion(f32[56,128,256]{2,1,0:T(8,128)} %get-tuple-element.3, f32[7168]{0:T(1024)S(1)} %broadcast_add_fusion), kind=kLoop, calls=%fused_computation.7 | loop fusion | flops 9175040 | bytes 11038720 | tf_op jit(solution)/shard_map/convert_element_type | solution.py:56
  123.1 0.0 reduce-scatter.4.cloned.1.call-update
  123.2 0.0 all-gather.3.cloned.1.call-start
  123.2 83.0 %reduce-scatter.4.cloned.1.call-done = bf16[224,256]{1,0:T(8,128)(2,1)} async-done(((bf16[7168,256]{1,0:T(8,128)(2,1)}), bf16[224,256]{1,0:T(8,128)(2,1)}) %reduce-scatter.4.cloned.1.call-update) | async-done | bytes 114704 | tf_op jit(solution)/shard_map/reduce_scatter | solution.py:56
  206.2 14.6 %fusion = bf16[32,256]{1,0:T(8,128)(2,1)S(1)} fusion(bf16[224,256]{1,0:T(8,128)(2,1)} %reduce-scatter.4.cloned.1.call-done), kind=kCustom, calls=%all-reduce-scatter | all-reduce-scatter fusion | flops 65537 | bytes 132096
  220.9 2.6 collective-permute-start
  223.5 0.1 dynamic_slice.3
  223.6 0.0 copy-done.3
  223.6 0.6 dynamic-slice.4
  224.8 0.6 collective-permute-done
  225.4 0.1 concatenate
  225.5 0.1 multiply_multiply_fusion
  225.6 0.6 fusion.13
  226.1 0.8 fusion.12
  227.0 0.0 all-gather.3.cloned.1.call-update
  227.0 121.3 %all-gather.3.cloned.1.call-done = bf16[256,28,256]{2,1,0:T(8,128)(2,1)} async-done(((bf16[1,28,256]{2,1,0:T(8,128)(2,1)}), bf16[256,28,256]{2,1,0:T(8,128)(2,1)}) %all-gather.3.cloned.1.call-update) | async-done | bytes 3670032 | tf_op jit(solution)/shard_map/all_gather | solution.py:62
  348.2 6.5 %reshape.810 = bf16[7168,256]{1,0:T(8,128)(2,1)} reshape(bf16[256,28,256]{2,1,0:T(8,128)(2,1)} %all-gather.3.cloned.1.call-done) | data formatting | bytes 7340032
  (13 shorter events, 0.1 us)
Async XLA Ops:
  7.2 0.9 copy-start
  7.2 199.0 %reduce-scatter.4.cloned.1.call-start = ((), (), s32[]{:S(2)}) async-start(), calls=%async_computation.1 | async-start | bytes 3784704 | tf_op jit(solution)/shard_map/reduce_scatter | solution.py:56
  17.8 8.4 %copy-start.1 = (s32[56,256]{1,0:T(8,128)S(1)}, s32[56,256]{1,0:T(8,128)}, u32[]{:S(2)}) copy-start(s32[56,256]{1,0:T(8,128)} %param.5) | copy-start | bytes 172036
  116.8 106.8 %copy-start.3 = (u32[256]{0:T(256)S(1)}, u32[256]{0:T(256)}, u32[]{:S(2)}) copy-start(u32[256]{0:T(256)} %constant.402) | copy-start | bytes 3076
  123.2 225.1 %all-gather.3.cloned.1.call-start = ((), (), s32[]{:S(2)}) async-start(), calls=%async_computation.2 | async-start | bytes 4210688 | tf_op jit(solution)/shard_map/all_gather | solution.py:62
  220.9 4.5 %collective-permute-start = (bf16[28,256]{1,0:T(8,128)(2,1)S(1)}, bf16[28,256]{1,0:T(8,128)(2,1)S(1)}, u32[]{:S(2)}, u32[]{:S(2)}) collective-permute-start(bf16[28,256]{1,0:T(8,128)(2,1)S(1)} %slice), channel_id=1, source_target_pairs={{0,1},{1,2},{2,3},{3,4},{4,5},{5,6},{6,7},{8,9},{9,10},{10,11},{11... | collective-permute-start | bytes 43016
  225.6 129.1 %copy-start.2 = (f32[28,256]{1,0:T(8,128)}, f32[28,256]{1,0:T(8,128)S(1)}, u32[]{:S(2)}) copy-start(f32[28,256]{1,0:T(8,128)S(1)} %multiply_multiply_fusion) | copy-start | bytes 86020
Sparse Core Ops, SparseCore 0:
  123.3 82.9 reduce-scatter.3
  227.1 121.0 all-gather.2
where the time goes:
time: 364 us; the launch traced here: 362 us
  waiting for transfers between devices  205 us (56%)
  blocking collectives  94.5 us (26%)
  matrix products  21.9 us (6%)
  local copies, waits for them, and re-layouts  16.5 us (5%)
  between operations  14.8 us (4%)
  other arithmetic  6.44 us (2%)
    all_gather x1, waiting for transfers between devices, body(): grad_mean = lax.all_gather(own_grad, ('node', 'outer'), axis=0, tiled=True)  121 us
    reduce_scatter x1, waiting for transfers between devices, body(): lax.psum_scatter(quant.astype(jnp.bfloat16), 'node', scatter_dimension=0,...  83 us
    pmax x1, blocking collectives, body(): largest = lax.pmax(jnp.max(jnp.abs(turned), axis=1), ('node', 'outer'))  79.8 us
    unnamed x1, blocking collectives  14.6 us
    dot_general x1, matrix products, rotate(): jnp.einsum('ij,bjc->bci', hadamard(BLK), blocks, precision=lax.Precision....  10.7 us
    dot_general x1, matrix products, body(): lax.dot_general(acts, cotangent, (((0,), (0,)), ((), ())), preferred_elem...  9.78 us
    reshape x1, local copies, waits for them, and re-layouts, rotate(): partial_value.reshape(BLOCKS, BLK, COLS)  8.4 us
    unnamed x12, local copies, waits for them, and re-layouts  7.98 us
  transfers between devices with their start and end apart: 3, of which 3 were waited for; matrix products, arithmetic and copies ran while one was open for 0% of the time, Pallas kernels for 0%

commit v1 on v0

v1 whole, which is shorter than its diff:
```python
import math

import jax
import jax.numpy as jnp
import numpy as np
from jax import lax
from jax.experimental import pallas as pl
from jax.experimental.pallas import tpu as pltpu
from jax.sharding import Mesh
from jax.sharding import PartitionSpec as P

COLS = 128
BLK = 256
LEVELS = 15
BLOCKS = 56
ROWS = BLOCKS * COLS
NX = 4
NY = 4
NZ = 8
PLANE = NX * NY
DEVICES = 256
CORE_ROWS = ROWS // (2 * PLANE)
OWN = ROWS // DEVICES
GROUP = 7
STEPS = BLOCKS // GROUP
PAIRS = PLANE // STEPS
VMEM_BYTES = 48 * 1024 * 1024


def hadamard(size):
    matrix = np.ones((1, 1), np.float32)
    while matrix.shape[0] < size:
        matrix = np.block([[matrix, matrix], [matrix, -matrix]])
    return matrix


HADAMARD = hadamard(BLK)


def rotate_kernel(core_ref, acts_ref, cot_ref, signs_ref, had_ref, keep_ref, give_ref, largest_ref, cot_t, turned_ref):
    step = pl.program_id(0)
    core = core_ref[0]

    @pl.when(step == 0)
    def _():
        cot_t[...] = cot_ref[...].T

    for b in range(GROUP):
        block = jnp.dot(
            cot_t[...], acts_ref[:, b * BLK : (b + 1) * BLK], preferred_element_type=jnp.float32
        )
        row = pl.ds(step * GROUP + b, 1)
        block = block * signs_ref[row, :].astype(jnp.float32)
        high = block.astype(jnp.bfloat16)
        low = (block - high.astype(jnp.float32)).astype(jnp.bfloat16)
        had = had_ref[...]
        turned = jnp.dot(high, had, preferred_element_type=jnp.float32)
        turned = turned + jnp.dot(low, had, preferred_element_type=jnp.float32)
        turned = turned * (1.0 / math.sqrt(BLK))
        turned_ref[b * COLS : (b + 1) * COLS, :] = turned
        size = jnp.abs(turned)
        size = jnp.maximum(size[:, :COLS], size[:, COLS:]).T
        largest_ref[row, :] = jnp.max(size, axis=0, keepdims=True)
    for pair in range(PAIRS):
        for ref, part in ((keep_ref, core), (give_ref, 1 - core)):
            start = pl.multiple_of((2 * pair + part) * CORE_ROWS, 8)
            ref[pair] = turned_ref[pl.ds(start, CORE_ROWS), :]


def rotate(core, acts, cotangent, signs, had):
    tokens = acts.shape[0]
    half = jax.ShapeDtypeStruct((PLANE, CORE_ROWS, BLK), jnp.float32)
    out_spec = pl.BlockSpec((PAIRS, CORE_ROWS, BLK), lambda i, core: (i, 0, 0))
    return pl.pallas_call(
        rotate_kernel,
        grid_spec=pltpu.PrefetchScalarGridSpec(
            num_scalar_prefetch=1,
            grid=(STEPS,),
            in_specs=[
                pl.BlockSpec((tokens, GROUP * BLK), lambda i, core: (0, i)),
                pl.BlockSpec((tokens, COLS), lambda i, core: (0, 0)),
                pl.BlockSpec((BLOCKS, BLK), lambda i, core: (0, 0)),
                pl.BlockSpec((BLK, BLK), lambda i, core: (0, 0)),
            ],
            out_specs=[
                out_spec,
                out_spec,
                pl.BlockSpec((BLOCKS, COLS), lambda i, core: (0, 0)),
            ],
            scratch_shapes=[
                pltpu.VMEM((COLS, tokens), jnp.bfloat16),
                pltpu.VMEM((GROUP * COLS, BLK), jnp.float32),
            ],
        ),
        out_shape=[half, half, jax.ShapeDtypeStruct((BLOCKS, COLS), jnp.float32)],
        compiler_params=pltpu.CompilerParams(vmem_limit_bytes=VMEM_BYTES),
        cost_estimate=pl.CostEstimate(
            flops=2 * ROWS * BLK * (tokens + 2 * BLK), bytes_accessed=17_000_000, transcendentals=0
        ),
    )(core, acts, cotangent, signs, had)


def quantize_kernel(core_ref, keep_ref, other_ref, scale_ref, sum_ref, factor):
    core = core_ref[0]
    first = pl.program_id(0) * GROUP
    for b in range(GROUP):
        row = LEVELS / scale_ref[pl.ds(first + b, 1), :]
        factor[b * COLS : (b + 1) * COLS, :] = jnp.broadcast_to(row, (COLS, COLS)).T
    for pair in range(PAIRS):
        start = pl.multiple_of((2 * pair + core) * CORE_ROWS, 8)
        scale = factor[pl.ds(start, CORE_ROWS), :]
        for lane in (0, COLS):
            mine = jnp.floor(keep_ref[pair, :, lane : lane + COLS] * scale + 0.5)
            other = jnp.floor(other_ref[pair, :, lane : lane + COLS] * scale + 0.5)
            sum_ref[pair, :, lane : lane + COLS] = (mine + other).astype(jnp.bfloat16)


def quantize(core, keep, other, scale):
    spec = pl.BlockSpec((PAIRS, CORE_ROWS, BLK), lambda i, core: (i, 0, 0))
    return pl.pallas_call(
        quantize_kernel,
        grid_spec=pltpu.PrefetchScalarGridSpec(
            num_scalar_prefetch=1,
            grid=(STEPS,),
            in_specs=[spec, spec, pl.BlockSpec((BLOCKS, COLS), lambda i, core: (0, 0))],
            out_specs=spec,
            scratch_shapes=[pltpu.VMEM((GROUP * COLS, COLS), jnp.float32)],
        ),
        out_shape=jax.ShapeDtypeStruct((PLANE, CORE_ROWS, BLK), jnp.bfloat16),
        compiler_params=pltpu.CompilerParams(vmem_limit_bytes=VMEM_BYTES),
        cost_estimate=pl.CostEstimate(
            flops=4 * ROWS * BLK, bytes_accessed=9_200_000, transcendentals=0
        ),
    )(core, keep, other, scale)


def row_signs(signs, first_row, count):
    row_ids = first_row + jnp.arange(count, dtype=jnp.int32)
    onehot = (row_ids[:, None] // COLS == jnp.arange(BLOCKS, dtype=jnp.int32)[None, :]).astype(
        jnp.float32
    )
    return jnp.dot(onehot, signs.astype(jnp.float32), precision=lax.Precision.HIGHEST)


def unrotate(values, signs, first_row):
    back = jnp.dot(values, jnp.asarray(HADAMARD), precision=lax.Precision.HIGHEST)
    signed = back * row_signs(signs, first_row, values.shape[0])
    return (signed * (1.0 / math.sqrt(BLK))).astype(jnp.bfloat16)


def shift(value, axis, size, step):
    return lax.ppermute(value, axis, [((i + step) % size, i) for i in range(size)])


def flip(value, axis, size, bit):
    return lax.ppermute(value, axis, [(i, i ^ bit) for i in range(size)])


def max_everywhere(value):
    value = jnp.maximum(value, flip(value, "c", 2, 1))
    for axis, size, steps in (
        ("x", NX, (1, 2, 3)),
        ("y", NY, (1, 2, 3)),
        ("z", NZ, (1, 7)),
        ("z", NZ, (3, 5)),
    ):
        got = [shift(value, axis, size, s) for s in steps]
        for g in got:
            value = jnp.maximum(value, g)
    return value


def body(acts, cotangent, signs):
    x, y, c, z = (lax.axis_index(a) for a in ("x", "y", "c", "z"))
    core = jnp.full((1,), c, jnp.int32)
    had = jnp.asarray(HADAMARD, jnp.bfloat16)
    keep, give, largest = rotate(core, acts, cotangent, signs, had)
    scale = max_everywhere(largest) + 1e-06
    other = flip(give, "c", 2, 1)
    parts = quantize(core, keep, other, scale)
    parts = lax.all_to_all(parts, ("x", "y"), 0, 0, tiled=True)
    value = jnp.sum(parts.astype(jnp.float32), axis=0).astype(jnp.bfloat16)
    got = [flip(value, "z", NZ, bit) for bit in (1, 2, 3)]
    value = value.astype(jnp.float32)
    for g in got:
        value = value + g.astype(jnp.float32)
    value = value.astype(jnp.bfloat16)
    value = value.astype(jnp.float32) + flip(value, "z", NZ, 4).astype(jnp.float32)
    first_row = ((x * NY + y) * 2 + c) * CORE_ROWS
    own_scale = lax.dynamic_slice_in_dim(scale.reshape(ROWS), first_row, CORE_ROWS, 0)
    mean = value * own_scale[:, None] / (LEVELS * DEVICES)
    rotated_mean = lax.dynamic_slice_in_dim(mean, z * OWN, OWN, 0)
    grad = unrotate(mean, signs, first_row)
    grad = jnp.broadcast_to(grad[None], (PLANE, CORE_ROWS, BLK))
    grad = lax.all_to_all(grad, ("x", "y"), 0, 0, tiled=True)
    other = flip(grad, "c", 2, 1)
    first = jnp.where(c == 0, grad, other)
    second = jnp.where(c == 0, other, grad)
    grad_mean = jnp.stack([first, second], axis=1).reshape(ROWS, BLK)
    return (rotated_mean, grad_mean)


def solution(mesh):
    fine = Mesh(mesh.devices.reshape(NX, NY, 2, NZ), ("x", "y", "c", "z"))
    rows = ("x", "y", "c", "z")
    in_specs = (P(rows, None), P(rows, None), P())
    out_specs = (P(rows, None), P())
    return jax.shard_map(body, mesh=fine, in_specs=in_specs, out_specs=out_specs, check_vma=False)
```

time: 364 us -> 139 us (0.38)
  waiting for transfers between devices: 205 us -> 37.8 us
  blocking collectives: 94.5 us -> 40.8 us
  starting transfers between devices: 2.63 us -> 32.1 us
  matrix products: 21.9 us -> 0.65 us
  Pallas kernels: 0 us -> 17 us
  between operations: 14.8 us -> 0.76 us
  local copies, waits for them, and re-layouts: 16.5 us -> 5.32 us
    all_gather x1 -> x0, waiting for transfers between devices: 121 us -> none  [body(): grad_mean = lax.all_gather(own_grad, ('node', 'outer'), axis=0, tiled=True)]
    reduce_scatter x1 -> x0, waiting for transfers between devices: 83 us -> none  [body(): lax.psum_scatter(quant.astype(jnp.bfloat16), 'node', scatter_dimension=0,...]
    pmax x1 -> x0, blocking collectives: 79.8 us -> none  [body(): largest = lax.pmax(jnp.max(jnp.abs(turned), axis=1), ('node', 'outer'))]
    all_to_all x0 -> x2, blocking collectives: none -> 40.8 us  [the longest x1 21.5 us: body(): parts = lax.all_to_all(parts, ('x', 'y'), 0, 0, tiled=True)]
    ppermute x0 -> x17, waiting for transfers between devices: none -> 37.8 us  [the longest x7 22.3 us: flip(): return lax.ppermute(value, axis, [(i, i ^ bit) for i in range(size)])]
    ppermute x0 -> x17, starting transfers between devices: none -> 32.1 us  [the longest x7 18.3 us: flip(): return lax.ppermute(value, axis, [(i, i ^ bit) for i in range(size)])]
    dot_general x3 -> x1, matrix products: 21.1 us -> 0.36 us  [unrotate(): jnp.dot(values, jnp.asarray(HADAMARD), precision=lax.Precision.HIGHEST)]
    pallas_call x0 -> x2, Pallas kernels: none -> 17 us  [the longest x1 11 us: rotate(): pl.pallas_call(rotate_kernel, grid_spec=pltpu.PrefetchScalarGridSpec(num_...]
  transfers between devices with their start and end apart: 3 -> 17, of which waited for: 3 -> 14; matrix products, arithmetic and copies ran while one was open for 0% -> 1% of each run, Pallas kernels for 0% -> 0%
where the time goes in v1:
time: 139 us
  blocking collectives  40.8 us (29%)
  waiting for transfers between devices  37.8 us (27%)
  starting transfers between devices  32.1 us (23%)
  Pallas kernels  17 us (12%)
  local copies, waits for them, and re-layouts  5.32 us (4%)
  other arithmetic  4.35 us (3%)
    ppermute x7, waiting for transfers between devices, flip(): return lax.ppermute(value, axis, [(i, i ^ bit) for i in range(size)])  22.3 us
    all_to_all x1, blocking collectives, body(): parts = lax.all_to_all(parts, ('x', 'y'), 0, 0, tiled=True)  21.5 us
    all_to_all x1, blocking collectives, body(): grad = lax.all_to_all(grad, ('x', 'y'), 0, 0, tiled=True)  19.4 us
    ppermute x7, starting transfers between devices, flip(): return lax.ppermute(value, axis, [(i, i ^ bit) for i in range(size)])  18.3 us
    ppermute x10, waiting for transfers between devices, shift(): lax.ppermute(value, axis, [((i + step) % size, i) for i in range(size)])  15.5 us
    ppermute x10, starting transfers between devices, shift(): lax.ppermute(value, axis, [((i + step) % size, i) for i in range(size)])  13.8 us
    pallas_call x1, Pallas kernels, rotate(): pl.pallas_call(rotate_kernel, grid_spec=pltpu.PrefetchScalarGridSpec(num_...  11 us
    pallas_call x1, Pallas kernels, quantize(): pl.pallas_call(quantize_kernel, grid_spec=pltpu.PrefetchScalarGridSpec(nu...  5.96 us
  transfers between devices with their start and end apart: 17, of which 14 were waited for; matrix products, arithmetic and copies ran while one was open for 1% of the time, Pallas kernels for 0%

profile of v1, /device:TPU:33, one launch (start us, length us, event | category | flops | bytes accessed | tf_op | source)
XLA Modules:
  0.0 138.7 jit_solution(16158202791986483422)
XLA Ops:
  3.2 11.0 %shard_map.68 = (f32[16,224,256]{2,1,0:T(8,128)S(1)}, f32[16,224,256]{2,1,0:T(8,128)}, f32[56,128]{1,0:T(8,128)S(1)}) custom-call(s32[1]{0:T(128)} %bitcast.core_ref, bf16[320,14336]{1,0:T(8,128)(2,1)} %acts_ref.1, bf16[320,128]{1,0:T(8,128)(2,1)S(1)} %copy-done.2, s32[56,256]{1,0:T(8,128)S(1)} %copy-done, bf16[256,256]{1,0:T(8,128)(2,1)S(1)} %copy-done.3), custom_call_target="tpu_custom_call" | custom-call | flops 3053453312 | bytes 17000000 | tf_op jit(solution)/shard_map/pallas_call | solution.py:74
  14.9 5.8 %collective-permute-done.1 = f32[56,128]{1,0:T(8,128)S(1)} collective-permute-done((f32[56,128]{1,0:T(8,128)S(1)}, f32[56,128]{1,0:T(8,128)S(1)}, u32[]{:S(2)}, u32[]{:S(2)}) %collective-permute-start.1) | collective-permute-done | bytes 28704 | tf_op jit(solution)/shard_map/ppermute | solution.py:156
  20.8 2.5 %collective-permute-start.2 = (f32[56,128]{1,0:T(8,128)S(1)}, f32[56,128]{1,0:T(8,128)S(1)}, u32[]{:S(2)}, u32[]{:S(2)}) collective-permute-start(f32[56,128]{1,0:T(8,128)S(1)} %max.33), channel_id=1, source_target_pairs={{64,0},{128,64},{192,128},{0,192},{65,1},{129,65},{193,129},{1,193... | collective-permute-start | bytes 86024 | tf_op jit(solution)/shard_map/ppermute | solution.py:152
  24.4 3.1 %collective-permute-done.3 = f32[56,128]{1,0:T(8,128)S(1)} collective-permute-done((f32[56,128]{1,0:T(8,128)S(1)}, f32[56,128]{1,0:T(8,128)S(1)}, u32[]{:S(2)}, u32[]{:S(2)}) %collective-permute-start.3) | collective-permute-done | bytes 28704 | tf_op jit(solution)/shard_map/ppermute | solution.py:152
  27.8 2.8 %collective-permute-start.5 = (f32[56,128]{1,0:T(8,128)S(1)}, f32[56,128]{1,0:T(8,128)S(1)}, u32[]{:S(2)}, u32[]{:S(2)}) collective-permute-start(f32[56,128]{1,0:T(8,128)S(1)} %maximum_maximum_fusion.2), channel_id=1, source_target_pairs={{16,0},{32,16},{48,32},{0,48},{17,1},{33,17},{49,33},{1,49},{18,2}... | collective-permute-start | bytes 86024 | tf_op jit(solution)/shard_map/ppermute | solution.py:152
  31.6 3.2 %collective-permute-done.6 = f32[56,128]{1,0:T(8,128)S(1)} collective-permute-done((f32[56,128]{1,0:T(8,128)S(1)}, f32[56,128]{1,0:T(8,128)S(1)}, u32[]{:S(2)}, u32[]{:S(2)}) %collective-permute-start.6) | collective-permute-done | bytes 28704 | tf_op jit(solution)/shard_map/ppermute | solution.py:152
  38.1 3.8 %collective-permute-done.9 = f32[56,128]{1,0:T(8,128)S(1)} collective-permute-done((f32[56,128]{1,0:T(8,128)S(1)}, f32[56,128]{1,0:T(8,128)S(1)}, u32[]{:S(2)}, u32[]{:S(2)}) %collective-permute-start.9) | collective-permute-done | bytes 28704 | tf_op jit(solution)/shard_map/ppermute | solution.py:152
  41.9 2.4 %collective-permute-start.10 = (f32[56,128]{1,0:T(8,128)S(1)}, f32[56,128]{1,0:T(8,128)S(1)}, u32[]{:S(2)}, u32[]{:S(2)}) collective-permute-start(f32[56,128]{1,0:T(8,128)S(1)} %maximum_maximum_fusion), channel_id=1, source_target_pairs={{3,0},{4,1},{5,2},{6,3},{7,4},{0,5},{1,6},{2,7},{11,8},{12,9},{13,... | collective-permute-start | bytes 86024 | tf_op jit(solution)/shard_map/ppermute | solution.py:152
  44.3 2.2 %collective-permute-start.11 = (f32[56,128]{1,0:T(8,128)S(1)}, f32[56,128]{1,0:T(8,128)S(1)}, u32[]{:S(2)}, u32[]{:S(2)}) collective-permute-start(f32[56,128]{1,0:T(8,128)S(1)} %maximum_maximum_fusion), channel_id=1, source_target_pairs={{5,0},{6,1},{7,2},{0,3},{1,4},{2,5},{3,6},{4,7},{13,8},{14,9},{15,... | collective-permute-start | bytes 86024 | tf_op jit(solution)/shard_map/ppermute | solution.py:152
  48.1 2.0 %collective-permute-done.11 = f32[56,128]{1,0:T(8,128)S(1)} collective-permute-done((f32[56,128]{1,0:T(8,128)S(1)}, f32[56,128]{1,0:T(8,128)S(1)}, u32[]{:S(2)}, u32[]{:S(2)}) %collective-permute-start.11) | collective-permute-done | bytes 28704 | tf_op jit(solution)/shard_map/ppermute | solution.py:152
  50.1 1.8 %copy-done.4 = f32[16,224,256]{2,1,0:T(8,128)} copy-done((f32[16,224,256]{2,1,0:T(8,128)}, f32[16,224,256]{2,1,0:T(8,128)S(1)}, u32[]{:S(2)}) %copy-start.4) | copy-done | bytes 3670040
  51.9 6.0 %shard_map.69 = bf16[16,224,256]{2,1,0:T(8,128)(2,1)S(1)} custom-call(s32[1]{0:T(128)} %bitcast.core_ref, f32[16,224,256]{2,1,0:T(8,128)S(1)} %get-tuple-element.5.keep_ref, f32[16,224,256]{2,1,0:T(8,128)} %copy-done.4, f32[56,128]{1,0:T(8,128)S(1)} %maximum_add_fusion.scale_ref), custom_call_target="tpu_custom_call" | custom-call | flops 7340032 | bytes 9200000 | tf_op jit(solution)/shard_map/pallas_call | solution.py:120
  57.9 21.5 %all_to_all.10 = bf16[16,224,256]{2,1,0:T(8,128)(2,1)S(1)} all-to-all(bf16[16,224,256]{2,1,0:T(8,128)(2,1)S(1)} %shard_map.69), channel_id=1, replica_groups=mesh['x'=4,'y'=4,'c'=2,'z'=8] {'x','y'}, dimensions={0} | all-to-all | bytes 3670016 | tf_op jit(solution)/shard_map/all_to_all | solution.py:181
  79.6 2.0 %collective-permute-start.12 = (bf16[224,256]{1,0:T(8,128)(2,1)S(1)}, bf16[224,256]{1,0:T(8,128)(2,1)S(1)}, u32[]{:S(2)}, u32[]{:S(2)}) collective-permute-start(bf16[224,256]{1,0:T(8,128)(2,1)S(1)} %reduce_sum.12), channel_id=1, source_target_pairs={{0,1},{1,0},{2,3},{3,2},{4,5},{5,4},{6,7},{7,6},{8,9},{9,8},{10,11... | collective-permute-start | bytes 344072 | tf_op jit(solution)/shard_map/ppermute | solution.py:156
  81.6 1.8 %collective-permute-start.13 = (bf16[224,256]{1,0:T(8,128)(2,1)S(1)}, bf16[224,256]{1,0:T(8,128)(2,1)S(1)}, u32[]{:S(2)}, u32[]{:S(2)}) collective-permute-start(bf16[224,256]{1,0:T(8,128)(2,1)S(1)} %reduce_sum.12), channel_id=1, source_target_pairs={{0,2},{1,3},{2,0},{3,1},{4,6},{5,7},{6,4},{7,5},{8,10},{9,11},{10,... | collective-permute-start | bytes 344072 | tf_op jit(solution)/shard_map/ppermute | solution.py:156
  84.1 3.4 %collective-permute-done.13 = bf16[224,256]{1,0:T(8,128)(2,1)S(1)} collective-permute-done((bf16[224,256]{1,0:T(8,128)(2,1)S(1)}, bf16[224,256]{1,0:T(8,128)(2,1)S(1)}, u32[]{:S(2)}, u32[]{:S(2)}) %collective-permute-start.13) | collective-permute-done | bytes 114720 | tf_op jit(solution)/shard_map/ppermute | solution.py:156
  87.4 1.9 %collective-permute-done.14 = bf16[224,256]{1,0:T(8,128)(2,1)S(1)} collective-permute-done((bf16[224,256]{1,0:T(8,128)(2,1)S(1)}, bf16[224,256]{1,0:T(8,128)(2,1)S(1)}, u32[]{:S(2)}, u32[]{:S(2)}) %collective-permute-start.14) | collective-permute-done | bytes 114720 | tf_op jit(solution)/shard_map/ppermute | solution.py:156
  89.3 2.2 %collective-permute-start.15 = (bf16[224,256]{1,0:T(8,128)(2,1)S(1)}, bf16[224,256]{1,0:T(8,128)(2,1)S(1)}, u32[]{:S(2)}, u32[]{:S(2)}) collective-permute-start(bf16[224,256]{1,0:T(8,128)(2,1)S(1)} %add_convert_fusion), channel_id=1, source_target_pairs={{0,4},{1,5},{2,6},{3,7},{4,0},{5,1},{6,2},{7,3},{8,12},{9,13},{10,... | collective-permute-start | bytes 344072 | tf_op jit(solution)/shard_map/ppermute | solution.py:156
  91.9 7.7 %collective-permute-done.15 = bf16[224,256]{1,0:T(8,128)(2,1)S(1)} collective-permute-done((bf16[224,256]{1,0:T(8,128)(2,1)S(1)}, bf16[224,256]{1,0:T(8,128)(2,1)S(1)}, u32[]{:S(2)}, u32[]{:S(2)}) %collective-permute-start.15) | collective-permute-done | bytes 114720 | tf_op jit(solution)/shard_map/ppermute | solution.py:156
  100.3 19.4 %all_to_all.11 = bf16[16,224,256]{2,1,0:T(8,128)(2,1)S(1)} all-to-all(bf16[16,224,256]{2,1,0:T(8,128)(2,1)S(1)} %broadcast_in_dim.5), channel_id=1, replica_groups=mesh['x'=4,'y'=4,'c'=2,'z'=8] {'x','y'}, dimensions={0} | all-to-all | bytes 3670016 | tf_op jit(solution)/shard_map/all_to_all | solution.py:195
  119.6 11.7 %collective-permute-start.16 = (bf16[16,224,256]{2,1,0:T(8,128)(2,1)S(1)}, bf16[16,224,256]{2,1,0:T(8,128)(2,1)}, u32[]{:S(2)}, u32[]{:S(2)}) collective-permute-start(bf16[16,224,256]{2,1,0:T(8,128)(2,1)S(1)} %all_to_all.11), channel_id=1, source_target_pairs={{0,8},{8,0},{1,9},{9,1},{2,10},{10,2},{3,11},{11,3},{4,12},{12,4},... | collective-permute-start | bytes 5505032 | tf_op jit(solution)/shard_map/ppermute | solution.py:156
  131.9 2.9 %collective-permute-done.16 = bf16[16,224,256]{2,1,0:T(8,128)(2,1)} collective-permute-done((bf16[16,224,256]{2,1,0:T(8,128)(2,1)S(1)}, bf16[16,224,256]{2,1,0:T(8,128)(2,1)}, u32[]{:S(2)}, u32[]{:S(2)}) %collective-permute-start.16) | collective-permute-done | bytes 1835040 | tf_op jit(solution)/shard_map/ppermute | solution.py:156
  134.8 1.7 %select_bitcast_fusion.1 = (bf16[16,1,224,256]{3,2,1,0:T(8,128)(2,1)S(1)}, bf16[16,1,224,256]{3,2,1,0:T(8,128)(2,1)S(1)}) fusion(bf16[16,224,256]{2,1,0:T(8,128)(2,1)S(1)} %all_to_all.11, bf16[16,224,256]{2,1,0:T(8,128)(2,1)} %collective-permute-done.16, pred[]{:T(512)S(6)} %eq.8), kind=kLoop, calls=%fused_computation.2 | loop fusion | flops 1835008 | bytes 7340033 | tf_op jit(solution)/shard_map/stack | solution.py:199
  136.6 2.2 %pad_maximum_fusion = bf16[16,2,224,256]{3,2,1,0:T(8,128)(2,1)} fusion(bf16[16,1,224,256]{3,2,1,0:T(8,128)(2,1)S(1)} %get-tuple-element.9, bf16[16,1,224,256]{3,2,1,0:T(8,128)(2,1)S(1)} %get-tuple-element.8), kind=kLoop, calls=%fused_computation | loop fusion | flops 1835008 | bytes 7340032 | tf_op jit(solution)/shard_map/stack | solution.py:199
  (42 shorter events, 13.2 us)
Async XLA Ops:
  0.6 0.8 copy-start
  1.5 0.9 copy-start.2
  2.3 0.9 copy-start.3
  14.3 35.8 %collective-permute-start = (f32[16,224,256]{2,1,0:T(8,128)}, f32[16,224,256]{2,1,0:T(8,128)S(1)}, u32[]{:S(2)}, u32[]{:S(2)}) collective-permute-start(f32[16,224,256]{2,1,0:T(8,128)} %get-tuple-element.6), channel_id=1, source_target_pairs={{0,8},{8,0},{1,9},{9,1},{2,10},{10,2},{3,11},{11,3},{4,12},{12,4},... | collective-permute-start | bytes 11010056 | tf_op jit(solution)/shard_map/ppermute | solution.py:156
  14.9 5.8 %collective-permute-start.1 = (f32[56,128]{1,0:T(8,128)S(1)}, f32[56,128]{1,0:T(8,128)S(1)}, u32[]{:S(2)}, u32[]{:S(2)}) collective-permute-start(f32[56,128]{1,0:T(8,128)S(1)} %get-tuple-element.7), channel_id=1, source_target_pairs={{0,8},{8,0},{1,9},{9,1},{2,10},{10,2},{3,11},{11,3},{4,12},{12,4},... | collective-permute-start | bytes 86024 | tf_op jit(solution)/shard_map/ppermute | solution.py:156
  20.8 3.6 %collective-permute-start.2 = (f32[56,128]{1,0:T(8,128)S(1)}, f32[56,128]{1,0:T(8,128)S(1)}, u32[]{:S(2)}, u32[]{:S(2)}) collective-permute-start(f32[56,128]{1,0:T(8,128)S(1)} %max.33), channel_id=1, source_target_pairs={{64,0},{128,64},{192,128},{0,192},{65,1},{129,65},{193,129},{1,193... | collective-permute-start | bytes 86024 | tf_op jit(solution)/shard_map/ppermute | solution.py:152
  23.2 4.2 %collective-permute-start.3 = (f32[56,128]{1,0:T(8,128)S(1)}, f32[56,128]{1,0:T(8,128)S(1)}, u32[]{:S(2)}, u32[]{:S(2)}) collective-permute-start(f32[56,128]{1,0:T(8,128)S(1)} %max.33), channel_id=1, source_target_pairs={{128,0},{192,64},{0,128},{64,192},{129,1},{193,65},{1,129},{65,193... | collective-permute-start | bytes 86024 | tf_op jit(solution)/shard_map/ppermute | solution.py:152
  23.8 4.0 %collective-permute-start.4 = (f32[56,128]{1,0:T(8,128)S(1)}, f32[56,128]{1,0:T(8,128)S(1)}, u32[]{:S(2)}, u32[]{:S(2)}) collective-permute-start(f32[56,128]{1,0:T(8,128)S(1)} %max.33), channel_id=1, source_target_pairs={{192,0},{0,64},{64,128},{128,192},{193,1},{1,65},{65,129},{129,193... | collective-permute-start | bytes 86024 | tf_op jit(solution)/shard_map/ppermute | solution.py:152
  27.8 3.9 %collective-permute-start.5 = (f32[56,128]{1,0:T(8,128)S(1)}, f32[56,128]{1,0:T(8,128)S(1)}, u32[]{:S(2)}, u32[]{:S(2)}) collective-permute-start(f32[56,128]{1,0:T(8,128)S(1)} %maximum_maximum_fusion.2), channel_id=1, source_target_pairs={{16,0},{32,16},{48,32},{0,48},{17,1},{33,17},{49,33},{1,49},{18,2}... | collective-permute-start | bytes 86024 | tf_op jit(solution)/shard_map/ppermute | solution.py:152
  30.6 4.2 %collective-permute-start.6 = (f32[56,128]{1,0:T(8,128)S(1)}, f32[56,128]{1,0:T(8,128)S(1)}, u32[]{:S(2)}, u32[]{:S(2)}) collective-permute-start(f32[56,128]{1,0:T(8,128)S(1)} %maximum_maximum_fusion.2), channel_id=1, source_target_pairs={{32,0},{48,16},{0,32},{16,48},{33,1},{49,17},{1,33},{17,49},{34,2}... | collective-permute-start | bytes 86024 | tf_op jit(solution)/shard_map/ppermute | solution.py:152
  30.9 4.2 %collective-permute-start.7 = (f32[56,128]{1,0:T(8,128)S(1)}, f32[56,128]{1,0:T(8,128)S(1)}, u32[]{:S(2)}, u32[]{:S(2)}) collective-permute-start(f32[56,128]{1,0:T(8,128)S(1)} %maximum_maximum_fusion.2), channel_id=1, source_target_pairs={{48,0},{0,16},{16,32},{32,48},{49,1},{1,17},{17,33},{33,49},{50,2}... | collective-permute-start | bytes 86024 | tf_op jit(solution)/shard_map/ppermute | solution.py:152
  35.1 3.0 %collective-permute-start.8 = (f32[56,128]{1,0:T(8,128)S(1)}, f32[56,128]{1,0:T(8,128)S(1)}, u32[]{:S(2)}, u32[]{:S(2)}) collective-permute-start(f32[56,128]{1,0:T(8,128)S(1)} %maximum_maximum_fusion.1), channel_id=1, source_target_pairs={{1,0},{2,1},{3,2},{4,3},{5,4},{6,5},{7,6},{0,7},{9,8},{10,9},{11,1... | collective-permute-start | bytes 86024 | tf_op jit(solution)/shard_map/ppermute | solution.py:152
  35.2 6.7 %collective-permute-start.9 = (f32[56,128]{1,0:T(8,128)S(1)}, f32[56,128]{1,0:T(8,128)S(1)}, u32[]{:S(2)}, u32[]{:S(2)}) collective-permute-start(f32[56,128]{1,0:T(8,128)S(1)} %maximum_maximum_fusion.1), channel_id=1, source_target_pairs={{7,0},{0,1},{1,2},{2,3},{3,4},{4,5},{5,6},{6,7},{15,8},{8,9},{9,10... | collective-permute-start | bytes 86024 | tf_op jit(solution)/shard_map/ppermute | solution.py:152
  41.9 6.1 %collective-permute-start.10 = (f32[56,128]{1,0:T(8,128)S(1)}, f32[56,128]{1,0:T(8,128)S(1)}, u32[]{:S(2)}, u32[]{:S(2)}) collective-permute-start(f32[56,128]{1,0:T(8,128)S(1)} %maximum_maximum_fusion), channel_id=1, source_target_pairs={{3,0},{4,1},{5,2},{6,3},{7,4},{0,5},{1,6},{2,7},{11,8},{12,9},{13,... | collective-permute-start | bytes 86024 | tf_op jit(solution)/shard_map/ppermute | solution.py:152
  44.3 5.8 %collective-permute-start.11 = (f32[56,128]{1,0:T(8,128)S(1)}, f32[56,128]{1,0:T(8,128)S(1)}, u32[]{:S(2)}, u32[]{:S(2)}) collective-permute-start(f32[56,128]{1,0:T(8,128)S(1)} %maximum_maximum_fusion), channel_id=1, source_target_pairs={{5,0},{6,1},{7,2},{0,3},{1,4},{2,5},{3,6},{4,7},{13,8},{14,9},{15,... | collective-permute-start | bytes 86024 | tf_op jit(solution)/shard_map/ppermute | solution.py:152
  50.1 1.8 %copy-start.4 = (f32[16,224,256]{2,1,0:T(8,128)}, f32[16,224,256]{2,1,0:T(8,128)S(1)}, u32[]{:S(2)}) copy-start(f32[16,224,256]{2,1,0:T(8,128)S(1)} %collective-permute-done.other_ref) | copy-start | bytes 11010052
  79.4 12.2 %copy-start.1 = (s32[56,256]{1,0:T(8,128)S(1)}, s32[56,256]{1,0:T(8,128)}, u32[]{:S(2)}) copy-start(s32[56,256]{1,0:T(8,128)} %signs_ref.1) | copy-start | bytes 172036
  79.4 20.4 %copy-start.5 = (f32[256,256]{1,0:T(8,128)S(1)}, f32[256,256]{1,0:T(8,128)}, u32[]{:S(2)}) copy-start(f32[256,256]{1,0:T(8,128)} %constant.60.clone) | copy-start | bytes 786436
  79.6 4.4 %collective-permute-start.12 = (bf16[224,256]{1,0:T(8,128)(2,1)S(1)}, bf16[224,256]{1,0:T(8,128)(2,1)S(1)}, u32[]{:S(2)}, u32[]{:S(2)}) collective-permute-start(bf16[224,256]{1,0:T(8,128)(2,1)S(1)} %reduce_sum.12), channel_id=1, source_target_pairs={{0,1},{1,0},{2,3},{3,2},{4,5},{5,4},{6,7},{7,6},{8,9},{9,8},{10,11... | collective-permute-start | bytes 344072 | tf_op jit(solution)/shard_map/ppermute | solution.py:156
  81.6 5.9 %collective-permute-start.13 = (bf16[224,256]{1,0:T(8,128)(2,1)S(1)}, bf16[224,256]{1,0:T(8,128)(2,1)S(1)}, u32[]{:S(2)}, u32[]{:S(2)}) collective-permute-start(bf16[224,256]{1,0:T(8,128)(2,1)S(1)} %reduce_sum.12), channel_id=1, source_target_pairs={{0,2},{1,3},{2,0},{3,1},{4,6},{5,7},{6,4},{7,5},{8,10},{9,11},{10,... | collective-permute-start | bytes 344072 | tf_op jit(solution)/shard_map/ppermute | solution.py:156
  83.4 5.9 %collective-permute-start.14 = (bf16[224,256]{1,0:T(8,128)(2,1)S(1)}, bf16[224,256]{1,0:T(8,128)(2,1)S(1)}, u32[]{:S(2)}, u32[]{:S(2)}) collective-permute-start(bf16[224,256]{1,0:T(8,128)(2,1)S(1)} %reduce_sum.12), channel_id=1, source_target_pairs={{0,3},{1,2},{2,1},{3,0},{4,7},{5,6},{6,5},{7,4},{8,11},{9,10},{10,... | collective-permute-start | bytes 344072 | tf_op jit(solution)/shard_map/ppermute | solution.py:156
  89.3 10.3 %collective-permute-start.15 = (bf16[224,256]{1,0:T(8,128)(2,1)S(1)}, bf16[224,256]{1,0:T(8,128)(2,1)S(1)}, u32[]{:S(2)}, u32[]{:S(2)}) collective-permute-start(bf16[224,256]{1,0:T(8,128)(2,1)S(1)} %add_convert_fusion), channel_id=1, source_target_pairs={{0,4},{1,5},{2,6},{3,7},{4,0},{5,1},{6,2},{7,3},{8,12},{9,13},{10,... | collective-permute-start | bytes 344072 | tf_op jit(solution)/shard_map/ppermute | solution.py:156
  119.6 15.2 %collective-permute-start.16 = (bf16[16,224,256]{2,1,0:T(8,128)(2,1)S(1)}, bf16[16,224,256]{2,1,0:T(8,128)(2,1)}, u32[]{:S(2)}, u32[]{:S(2)}) collective-permute-start(bf16[16,224,256]{2,1,0:T(8,128)(2,1)S(1)} %all_to_all.11), channel_id=1, source_target_pairs={{0,8},{8,0},{1,9},{9,1},{2,10},{10,2},{3,11},{11,3},{4,12},{12,4},... | collective-permute-start | bytes 5505032 | tf_op jit(solution)/shard_map/ppermute | solution.py:156

commit v2 on v1

v2 whole, which is shorter than its diff:
```python
import math

import jax
import jax.numpy as jnp
import numpy as np
from jax import lax
from jax.experimental import pallas as pl
from jax.experimental.pallas import tpu as pltpu
from jax.sharding import Mesh
from jax.sharding import PartitionSpec as P

COLS = 128
BLK = 256
LEVELS = 15
BLOCKS = 56
ROWS = BLOCKS * COLS
NX = 4
NY = 4
NZ = 8
PLANE = NX * NY
DEVICES = 256
CORE_ROWS = ROWS // (2 * PLANE)
OWN = ROWS // DEVICES
GROUP = 7
STEPS = BLOCKS // GROUP
PAIRS = PLANE // STEPS
WIDTH = GROUP * BLK
AHEAD = 3
ROTATE_VMEM = 44 * 1024 * 1024
KERNEL_VMEM = 24 * 1024 * 1024
IN_VMEM = pl.BlockSpec(memory_space=pltpu.VMEM)
IN_SMEM = pl.BlockSpec(memory_space=pltpu.SMEM)
IN_ANY = pl.BlockSpec(memory_space=pl.ANY)


def hadamard(size):
    matrix = np.ones((1, 1), np.float32)
    while matrix.shape[0] < size:
        matrix = np.block([[matrix, matrix], [matrix, -matrix]])
    return matrix


HADAMARD = hadamard(BLK)


def rotate_kernel(
    core_ref,
    acts_hbm,
    cot_hbm,
    signs_hbm,
    keep_ref,
    give_ref,
    largest_ref,
    acts_ref,
    cot_ref,
    signs_ref,
    had_ref,
    cot_t,
    even_terms,
    odd_terms,
    turned_ref,
    sems,
    small_sems,
):
    core = core_ref[0]
    small = [
        pltpu.make_async_copy(source, target, small_sems.at[i])
        for i, (source, target) in enumerate(((cot_hbm, cot_ref), (signs_hbm, signs_ref)))
    ]

    def fetch(i):
        columns = pl.ds(pl.multiple_of(i * WIDTH, WIDTH), WIDTH)
        return pltpu.make_async_copy(acts_hbm.at[:, columns], acts_ref.at[i], sems.at[i])

    for copy in small:
        copy.start()
    for i in range(AHEAD):
        fetch(i).start()
    had = lax.broadcasted_iota(jnp.int32, (BLK, BLK), 0) & lax.broadcasted_iota(
        jnp.int32, (BLK, BLK), 1
    )
    for half in (4, 2, 1):
        had = had ^ (had >> half)
    had = (1 - 2 * (had & 1)).astype(jnp.float32) * (1.0 / math.sqrt(BLK))
    had = had.astype(jnp.bfloat16)
    had_ref[:BLK, :] = had
    had_ref[BLK:, :] = had
    for copy in small:
        copy.wait()
    cot_t[...] = cot_ref[...].T

    def arrive(i):
        fetch(i).wait()

        @pl.when(i + AHEAD < STEPS)
        def _():
            fetch(i + AHEAD).start()

    def multiply(i, b, terms):
        block = jnp.dot(
            cot_t[...], acts_ref[i, :, b * BLK : (b + 1) * BLK], preferred_element_type=jnp.float32
        )
        block = block * signs_ref[pl.ds(i * GROUP + b, 1), :].astype(jnp.float32)
        high = block.astype(jnp.bfloat16)
        low = (block - high.astype(jnp.float32)).astype(jnp.bfloat16)
        terms[b * COLS : (b + 1) * COLS, :BLK] = high
        terms[b * COLS : (b + 1) * COLS, BLK:] = low

    def turn(i, b, terms):
        turned = jnp.dot(
            terms[b * COLS : (b + 1) * COLS, :], had_ref[...], preferred_element_type=jnp.float32
        )
        turned_ref[b * COLS : (b + 1) * COLS, :] = turned
        size = jnp.abs(turned)
        size = jnp.maximum(size[:, :COLS], size[:, COLS:]).T
        largest_ref[pl.ds(i * GROUP + b, 1), :] = jnp.max(size, axis=0, keepdims=True)

    def hand_out(i):
        for pair in range(PAIRS):
            for ref, part in ((keep_ref, core), (give_ref, 1 - core)):
                start = pl.multiple_of((2 * pair + part) * CORE_ROWS, 8)
                ref[i * PAIRS + pair] = turned_ref[pl.ds(start, CORE_ROWS), :]

    def both(i, terms, next_terms):
        arrive(i + 1)
        for b in range(GROUP):
            multiply(i + 1, b, next_terms)
            turn(i, b, terms)
        hand_out(i)

    arrive(0)
    for b in range(GROUP):
        multiply(0, b, even_terms)

    def two_steps(k, carry):
        both(2 * k, even_terms, odd_terms)
        both(2 * k + 1, odd_terms, even_terms)
        return carry

    lax.fori_loop(0, STEPS // 2 - 1, two_steps, 0)
    both(STEPS - 2, even_terms, odd_terms)
    for b in range(GROUP):
        turn(STEPS - 1, b, odd_terms)
    hand_out(STEPS - 1)


def rotate(core, acts, cotangent, signs):
    tokens = acts.shape[0]
    half = jax.ShapeDtypeStruct((PLANE, CORE_ROWS, BLK), jnp.float32)
    return pl.pallas_call(
        rotate_kernel,
        in_specs=[IN_SMEM, IN_ANY, IN_ANY, IN_ANY],
        out_specs=[IN_VMEM, IN_VMEM, IN_VMEM],
        out_shape=[half, half, jax.ShapeDtypeStruct((BLOCKS, COLS), jnp.float32)],
        scratch_shapes=[
            pltpu.VMEM((STEPS, tokens, WIDTH), jnp.bfloat16),
            pltpu.VMEM((tokens, COLS), jnp.bfloat16),
            pltpu.VMEM((BLOCKS, BLK), jnp.int32),
            pltpu.VMEM((2 * BLK, BLK), jnp.bfloat16),
            pltpu.VMEM((COLS, tokens), jnp.bfloat16),
            pltpu.VMEM((GROUP * COLS, 2 * BLK), jnp.bfloat16),
            pltpu.VMEM((GROUP * COLS, 2 * BLK), jnp.bfloat16),
            pltpu.VMEM((GROUP * COLS, BLK), jnp.float32),
            pltpu.SemaphoreType.DMA((STEPS,)),
            pltpu.SemaphoreType.DMA((2,)),
        ],
        compiler_params=pltpu.CompilerParams(vmem_limit_bytes=ROTATE_VMEM),
        cost_estimate=pl.CostEstimate(
            flops=2 * ROWS * BLK * (tokens + 2 * BLK), bytes_accessed=17_000_000, transcendentals=0
        ),
    )(core, acts, cotangent, signs)


def quantize_kernel(core_ref, keep_ref, other_ref, scale_ref, sum_ref, factor):
    core = core_ref[0]

    def step(i, carry):
        for b in range(GROUP):
            row = LEVELS / scale_ref[pl.ds(i * GROUP + b, 1), :]
            factor[b * COLS : (b + 1) * COLS, :] = jnp.broadcast_to(row, (COLS, COLS)).T
        for pair in range(PAIRS):
            start = pl.multiple_of((2 * pair + core) * CORE_ROWS, 8)
            scale = factor[pl.ds(start, CORE_ROWS), :]
            j = i * PAIRS + pair
            for lane in (0, COLS):
                mine = jnp.floor(keep_ref[j, :, lane : lane + COLS] * scale + 0.5)
                other = jnp.floor(other_ref[j, :, lane : lane + COLS] * scale + 0.5)
                sum_ref[j, :, lane : lane + COLS] = (mine + other).astype(jnp.bfloat16)
        return carry

    lax.fori_loop(0, STEPS, step, 0)


def quantize(core, keep, other, scale):
    return pl.pallas_call(
        quantize_kernel,
        in_specs=[IN_SMEM, IN_VMEM, IN_VMEM, IN_VMEM],
        out_specs=IN_VMEM,
        out_shape=jax.ShapeDtypeStruct((PLANE, CORE_ROWS, BLK), jnp.bfloat16),
        scratch_shapes=[pltpu.VMEM((GROUP * COLS, COLS), jnp.float32)],
        compiler_params=pltpu.CompilerParams(vmem_limit_bytes=KERNEL_VMEM),
        cost_estimate=pl.CostEstimate(
            flops=4 * ROWS * BLK, bytes_accessed=9_200_000, transcendentals=0
        ),
    )(core, keep, other, scale)


def place_kernel(core_ref, part_ref, whole_ref, sem):
    copies = [
        pltpu.make_async_copy(part_ref.at[i], whole_ref.at[i, core_ref[0]], sem.at[i])
        for i in range(PLANE)
    ]
    for copy in copies:
        copy.start()
    for copy in copies:
        copy.wait()


def place(core, part):
    return pl.pallas_call(
        place_kernel,
        in_specs=[IN_SMEM, IN_VMEM],
        out_specs=IN_ANY,
        out_shape=jax.ShapeDtypeStruct((PLANE, 2, CORE_ROWS, BLK), jnp.bfloat16),
        scratch_shapes=[pltpu.SemaphoreType.DMA((PLANE,))],
        compiler_params=pltpu.CompilerParams(vmem_limit_bytes=KERNEL_VMEM),
        cost_estimate=pl.CostEstimate(flops=0, bytes_accessed=3_700_000, transcendentals=0),
    )(core, part)


def row_signs(signs, first_row, count):
    row_ids = first_row + jnp.arange(count, dtype=jnp.int32)
    onehot = (row_ids[:, None] // COLS == jnp.arange(BLOCKS, dtype=jnp.int32)[None, :]).astype(
        jnp.float32
    )
    return jnp.dot(onehot, signs.astype(jnp.float32), precision=lax.Precision.HIGHEST)


def unrotate(values, signs, first_row):
    back = jnp.dot(values, jnp.asarray(HADAMARD), precision=lax.Precision.HIGHEST)
    signed = back * row_signs(signs, first_row, values.shape[0])
    return (signed * (1.0 / math.sqrt(BLK))).astype(jnp.bfloat16)


def shift(value, axis, size, step):
    return lax.ppermute(value, axis, [((i + step) % size, i) for i in range(size)])


def flip(value, axis, size, bit):
    return lax.ppermute(value, axis, [(i, i ^ bit) for i in range(size)])


def mirror(value, axis, size):
    return lax.ppermute(value, axis, [(i, size - 1 - i) for i in range(size)])


def max_everywhere(value):
    for axis, size, steps in (
        ("x", NX, (1, 2, 3)),
        ("y", NY, (1, 2, 3)),
        ("z", NZ, (1, 7)),
        ("z", NZ, (3, 5)),
    ):
        got = [shift(value, axis, size, s) for s in steps]
        for g in got:
            value = jnp.maximum(value, g)
    return value


def sum_z(value):
    got = [flip(value, "z", NZ, bit) for bit in (1, 2, 3)]
    value = value.astype(jnp.float32)
    for g in got:
        value = value + g.astype(jnp.float32)
    value = value.astype(jnp.bfloat16)
    return value.astype(jnp.float32) + mirror(value, "z", NZ).astype(jnp.float32)


def body(acts, cotangent, signs):
    x, y, c, z = (lax.axis_index(a) for a in ("x", "y", "c", "z"))
    core = jnp.full((1,), c, jnp.int32)
    keep, give, largest = rotate(core, acts, cotangent, signs)
    beside = flip(largest, "c", 2, 1)
    give, beside = lax.optimization_barrier((give, beside))
    other = flip(give, "c", 2, 1)
    scale = max_everywhere(jnp.maximum(largest, beside)) + 1e-06
    parts = quantize(core, keep, other, scale)
    parts = lax.all_to_all(parts, ("x", "y"), 0, 0, tiled=True)
    value = jnp.sum(parts.astype(jnp.float32), axis=0).astype(jnp.bfloat16)
    value = sum_z(value)
    first_row = ((x * NY + y) * 2 + c) * CORE_ROWS
    own_scale = lax.dynamic_slice_in_dim(scale.reshape(ROWS), first_row, CORE_ROWS, 0)
    mean = value * own_scale[:, None] / (LEVELS * DEVICES)
    rotated_mean = lax.dynamic_slice_in_dim(mean, z * OWN, OWN, 0)
    grad = unrotate(mean, signs, first_row)
    grad = jnp.broadcast_to(grad[None], (PLANE, CORE_ROWS, BLK))
    grad = lax.all_to_all(grad, ("x", "y"), 0, 0, tiled=True)
    whole = place(core, grad)
    other = flip(grad, "c", 2, 1)
    grad_mean = lax.dynamic_update_slice_in_dim(whole, other[:, None], 1 - c, 1)
    return (rotated_mean, grad_mean.reshape(ROWS, BLK))


def solution(mesh):
    fine = Mesh(mesh.devices.reshape(NX, NY, 2, NZ), ("x", "y", "c", "z"))
    rows = ("x", "y", "c", "z")
    in_specs = (P(rows, None), P(rows, None), P())
    out_specs = (P(rows, None), P())
    return jax.shard_map(body, mesh=fine, in_specs=in_specs, out_specs=out_specs, check_vma=False)
```

time: 139 us -> 120 us (0.86)
  waiting for transfers between devices: 37.8 us -> 29.8 us
  Pallas kernels: 17 us -> 11.5 us
  other arithmetic: 4.35 us -> 0.46 us
  starting transfers between devices: 32.1 us -> 30.2 us
    ppermute x7 -> x6, waiting for transfers between devices: 22.3 us -> 8.27 us  [flip(): return lax.ppermute(value, axis, [(i, i ^ bit) for i in range(size)])]
    ppermute x0 -> x1, waiting for transfers between devices: none -> 6.07 us  [mirror(): return lax.ppermute(value, axis, [(i, size - 1 - i) for i in range(size)])]
    pallas_call x2 -> x3, Pallas kernels: 17 us -> 11.5 us  [the longest x1 7.36 us: rotate(): pl.pallas_call(rotate_kernel, in_specs=[IN_SMEM, IN_ANY, IN_ANY, IN_ANY],...]
    another operation x2 -> x0, other arithmetic: 3.89 us -> none  [body(): grad_mean = jnp.stack([first, second], axis=1).reshape(ROWS, BLK)]
    ppermute x7 -> x6, starting transfers between devices: 18.3 us -> 15.1 us  [flip(): return lax.ppermute(value, axis, [(i, i ^ bit) for i in range(size)])]
    dynamic_update_slice x0 -> x1, local copies, waits for them, and re-layouts: none -> 2.84 us  [body(): grad_mean = lax.dynamic_update_slice_in_dim(whole, other[:, None], 1 - c, 1)]
    unnamed x12 -> x8, local copies, waits for them, and re-layouts: 4.44 us -> 1.71 us
  transfers between devices with their start and end apart: 17 -> 17, of which waited for: 14 -> 14; matrix products, arithmetic and copies ran while one was open for 1% -> 1% of each run, Pallas kernels for 0% -> 1%
where the time goes in v2:
time: 120 us
  blocking collectives  41.3 us (34%)
  starting transfers between devices  30.2 us (25%)
  waiting for transfers between devices  29.8 us (25%)
  Pallas kernels  11.5 us (10%)
  local copies, waits for them, and re-layouts  5.43 us (5%)
    all_to_all x1, blocking collectives, body(): parts = lax.all_to_all(parts, ('x', 'y'), 0, 0, tiled=True)  21.6 us
    all_to_all x1, blocking collectives, body(): grad = lax.all_to_all(grad, ('x', 'y'), 0, 0, tiled=True)  19.7 us
    ppermute x10, waiting for transfers between devices, shift(): lax.ppermute(value, axis, [((i + step) % size, i) for i in range(size)])  15.4 us
    ppermute x6, starting transfers between devices, flip(): return lax.ppermute(value, axis, [(i, i ^ bit) for i in range(size)])  15.1 us
    ppermute x10, starting transfers between devices, shift(): lax.ppermute(value, axis, [((i + step) % size, i) for i in range(size)])  13.8 us
    ppermute x6, waiting for transfers between devices, flip(): return lax.ppermute(value, axis, [(i, i ^ bit) for i in range(size)])  8.27 us
    pallas_call x1, Pallas kernels, rotate(): pl.pallas_call(rotate_kernel, in_specs=[IN_SMEM, IN_ANY, IN_ANY, IN_ANY],...  7.36 us
    ppermute x1, waiting for transfers between devices, mirror(): return lax.ppermute(value, axis, [(i, size - 1 - i) for i in range(size)])  6.07 us
  transfers between devices with their start and end apart: 17, of which 14 were waited for; matrix products, arithmetic and copies ran while one was open for 1% of the time, Pallas kernels for 1%

profile of v2, /device:TPU:33, one launch (start us, length us, event | category | flops | bytes accessed | tf_op | source)
XLA Modules:
  0.0 120.1 jit_solution(8297211983553906344)
XLA Ops:
  2.3 7.4 %shard_map.59 = (f32[16,224,256]{2,1,0:T(8,128)S(1)}, f32[16,224,256]{2,1,0:T(8,128)S(1)}, f32[56,128]{1,0:T(8,128)S(1)}) custom-call(s32[1]{0:T(128)} %bitcast.core_ref, bf16[320,14336]{1,0:T(8,128)(2,1)} %acts_hbm.1, bf16[320,128]{1,0:T(8,128)(2,1)S(1)} %copy-done.2, s32[56,256]{1,0:T(8,128)S(1)} %copy-done), custom_call_target="tpu_custom_call" | custom-call | flops 3053453312 | bytes 17000000 | tf_op jit(solution)/shard_map/pallas_call | solution.py:150
  11.7 2.5 %collective-permute-start.2 = (f32[56,128]{1,0:T(8,128)S(1)}, f32[56,128]{1,0:T(8,128)S(1)}, u32[]{:S(2)}, u32[]{:S(2)}) collective-permute-start(f32[56,128]{1,0:T(8,128)S(1)} %max.33), channel_id=1, source_target_pairs={{64,0},{128,64},{192,128},{0,192},{65,1},{129,65},{193,129},{1,193... | collective-permute-start | bytes 86024 | tf_op jit(solution)/shard_map/ppermute | solution.py:246
  15.3 3.1 %collective-permute-done.3 = f32[56,128]{1,0:T(8,128)S(1)} collective-permute-done((f32[56,128]{1,0:T(8,128)S(1)}, f32[56,128]{1,0:T(8,128)S(1)}, u32[]{:S(2)}, u32[]{:S(2)}) %collective-permute-start.3) | collective-permute-done | bytes 28704 | tf_op jit(solution)/shard_map/ppermute | solution.py:246
  18.7 2.8 %collective-permute-start.5 = (f32[56,128]{1,0:T(8,128)S(1)}, f32[56,128]{1,0:T(8,128)S(1)}, u32[]{:S(2)}, u32[]{:S(2)}) collective-permute-start(f32[56,128]{1,0:T(8,128)S(1)} %maximum_maximum_fusion.2), channel_id=1, source_target_pairs={{16,0},{32,16},{48,32},{0,48},{17,1},{33,17},{49,33},{1,49},{18,2}... | collective-permute-start | bytes 86024 | tf_op jit(solution)/shard_map/ppermute | solution.py:246
  22.6 3.2 %collective-permute-done.6 = f32[56,128]{1,0:T(8,128)S(1)} collective-permute-done((f32[56,128]{1,0:T(8,128)S(1)}, f32[56,128]{1,0:T(8,128)S(1)}, u32[]{:S(2)}, u32[]{:S(2)}) %collective-permute-start.6) | collective-permute-done | bytes 28704 | tf_op jit(solution)/shard_map/ppermute | solution.py:246
  26.2 1.7 %collective-permute-start.9 = (f32[56,128]{1,0:T(8,128)S(1)}, f32[56,128]{1,0:T(8,128)S(1)}, u32[]{:S(2)}, u32[]{:S(2)}) collective-permute-start(f32[56,128]{1,0:T(8,128)S(1)} %maximum_maximum_fusion.1), channel_id=1, source_target_pairs={{7,0},{0,1},{1,2},{2,3},{3,4},{4,5},{5,6},{6,7},{15,8},{8,9},{9,10... | collective-permute-start | bytes 86024 | tf_op jit(solution)/shard_map/ppermute | solution.py:246
  29.1 3.8 %collective-permute-done.9 = f32[56,128]{1,0:T(8,128)S(1)} collective-permute-done((f32[56,128]{1,0:T(8,128)S(1)}, f32[56,128]{1,0:T(8,128)S(1)}, u32[]{:S(2)}, u32[]{:S(2)}) %collective-permute-start.9) | collective-permute-done | bytes 28704 | tf_op jit(solution)/shard_map/ppermute | solution.py:246
  32.9 2.4 %collective-permute-start.10 = (f32[56,128]{1,0:T(8,128)S(1)}, f32[56,128]{1,0:T(8,128)S(1)}, u32[]{:S(2)}, u32[]{:S(2)}) collective-permute-start(f32[56,128]{1,0:T(8,128)S(1)} %maximum_maximum_fusion), channel_id=1, source_target_pairs={{3,0},{4,1},{5,2},{6,3},{7,4},{0,5},{1,6},{2,7},{11,8},{12,9},{13,... | collective-permute-start | bytes 86024 | tf_op jit(solution)/shard_map/ppermute | solution.py:246
  35.2 2.2 %collective-permute-start.11 = (f32[56,128]{1,0:T(8,128)S(1)}, f32[56,128]{1,0:T(8,128)S(1)}, u32[]{:S(2)}, u32[]{:S(2)}) collective-permute-start(f32[56,128]{1,0:T(8,128)S(1)} %maximum_maximum_fusion), channel_id=1, source_target_pairs={{5,0},{6,1},{7,2},{0,3},{1,4},{2,5},{3,6},{4,7},{13,8},{14,9},{15,... | collective-permute-start | bytes 86024 | tf_op jit(solution)/shard_map/ppermute | solution.py:246
  37.4 1.6 %collective-permute-done.10 = f32[56,128]{1,0:T(8,128)S(1)} collective-permute-done((f32[56,128]{1,0:T(8,128)S(1)}, f32[56,128]{1,0:T(8,128)S(1)}, u32[]{:S(2)}, u32[]{:S(2)}) %collective-permute-start.10) | collective-permute-done | bytes 28704 | tf_op jit(solution)/shard_map/ppermute | solution.py:246
  39.0 2.0 %collective-permute-done.11 = f32[56,128]{1,0:T(8,128)S(1)} collective-permute-done((f32[56,128]{1,0:T(8,128)S(1)}, f32[56,128]{1,0:T(8,128)S(1)}, u32[]{:S(2)}, u32[]{:S(2)}) %collective-permute-start.11) | collective-permute-done | bytes 28704 | tf_op jit(solution)/shard_map/ppermute | solution.py:246
  41.0 2.8 %shard_map.60 = bf16[16,224,256]{2,1,0:T(8,128)(2,1)S(1)} custom-call(s32[1]{0:T(128)} %bitcast.core_ref, f32[16,224,256]{2,1,0:T(8,128)S(1)} %get-tuple-element.7.keep_ref, f32[16,224,256]{2,1,0:T(8,128)S(1)} %collective-permute-done.1.other_ref, f32[56,128]{1,0:T(8,128)S(1)} %maximum_add_fusion.scale_ref), custom_call_target="tpu_custom_call" | custom-call | flops 7340032 | bytes 9200000 | tf_op jit(solution)/shard_map/pallas_call | solution.py:195
  43.9 21.6 %all_to_all.10 = bf16[16,224,256]{2,1,0:T(8,128)(2,1)S(1)} all-to-all(bf16[16,224,256]{2,1,0:T(8,128)(2,1)S(1)} %shard_map.60), channel_id=1, replica_groups=mesh['x'=4,'y'=4,'c'=2,'z'=8] {'x','y'}, dimensions={0} | all-to-all | bytes 3670016 | tf_op jit(solution)/shard_map/all_to_all | solution.py:288
  65.7 2.0 %collective-permute-start.12 = (bf16[224,256]{1,0:T(8,128)(2,1)S(1)}, bf16[224,256]{1,0:T(8,128)(2,1)S(1)}, u32[]{:S(2)}, u32[]{:S(2)}) collective-permute-start(bf16[224,256]{1,0:T(8,128)(2,1)S(1)} %reduce_sum.12), channel_id=1, source_target_pairs={{0,1},{1,0},{2,3},{3,2},{4,5},{5,4},{6,7},{7,6},{8,9},{9,8},{10,11... | collective-permute-start | bytes 344072 | tf_op jit(solution)/shard_map/ppermute | solution.py:250
  67.7 1.8 %collective-permute-start.13 = (bf16[224,256]{1,0:T(8,128)(2,1)S(1)}, bf16[224,256]{1,0:T(8,128)(2,1)S(1)}, u32[]{:S(2)}, u32[]{:S(2)}) collective-permute-start(bf16[224,256]{1,0:T(8,128)(2,1)S(1)} %reduce_sum.12), channel_id=1, source_target_pairs={{0,2},{1,3},{2,0},{3,1},{4,6},{5,7},{6,4},{7,5},{8,10},{9,11},{10,... | collective-permute-start | bytes 344072 | tf_op jit(solution)/shard_map/ppermute | solution.py:250
  70.1 3.3 %collective-permute-done.13 = bf16[224,256]{1,0:T(8,128)(2,1)S(1)} collective-permute-done((bf16[224,256]{1,0:T(8,128)(2,1)S(1)}, bf16[224,256]{1,0:T(8,128)(2,1)S(1)}, u32[]{:S(2)}, u32[]{:S(2)}) %collective-permute-start.13) | collective-permute-done | bytes 114720 | tf_op jit(solution)/shard_map/ppermute | solution.py:250
  73.5 1.9 %collective-permute-done.14 = bf16[224,256]{1,0:T(8,128)(2,1)S(1)} collective-permute-done((bf16[224,256]{1,0:T(8,128)(2,1)S(1)}, bf16[224,256]{1,0:T(8,128)(2,1)S(1)}, u32[]{:S(2)}, u32[]{:S(2)}) %collective-permute-start.14) | collective-permute-done | bytes 114720 | tf_op jit(solution)/shard_map/ppermute | solution.py:250
  75.4 1.3 %collective-permute-start.15 = (bf16[224,256]{1,0:T(8,128)(2,1)S(1)}, bf16[224,256]{1,0:T(8,128)(2,1)S(1)}, u32[]{:S(2)}, u32[]{:S(2)}) collective-permute-start(bf16[224,256]{1,0:T(8,128)(2,1)S(1)} %add_convert_fusion), channel_id=1, source_target_pairs={{0,7},{1,6},{2,5},{3,4},{4,3},{5,2},{6,1},{7,0},{8,15},{9,14},{10,... | collective-permute-start | bytes 344072 | tf_op jit(solution)/shard_map/ppermute | solution.py:254
  77.1 6.1 %collective-permute-done.15 = bf16[224,256]{1,0:T(8,128)(2,1)S(1)} collective-permute-done((bf16[224,256]{1,0:T(8,128)(2,1)S(1)}, bf16[224,256]{1,0:T(8,128)(2,1)S(1)}, u32[]{:S(2)}, u32[]{:S(2)}) %collective-permute-start.15) | collective-permute-done | bytes 114720 | tf_op jit(solution)/shard_map/ppermute | solution.py:254
  83.8 19.7 %all_to_all.11.part_ref = bf16[16,224,256]{2,1,0:T(8,128)(2,1)S(1)} all-to-all(bf16[16,224,256]{2,1,0:T(8,128)(2,1)S(1)} %broadcast_in_dim.7), channel_id=1, replica_groups=mesh['x'=4,'y'=4,'c'=2,'z'=8] {'x','y'}, dimensions={0} | all-to-all | bytes 3670016 | tf_op jit(solution)/shard_map/all_to_all | solution.py:297
  103.6 10.2 %collective-permute-start.16 = (bf16[16,224,256]{2,1,0:T(8,128)(2,1)S(1)}, bf16[16,224,256]{2,1,0:T(8,128)(2,1)}, u32[]{:S(2)}, u32[]{:S(2)}) collective-permute-start(bf16[16,224,256]{2,1,0:T(8,128)(2,1)S(1)} %all_to_all.11.part_ref), channel_id=1, source_target_pairs={{0,8},{8,0},{1,9},{9,1},{2,10},{10,2},{3,11},{11,3},{4,12},{12,4},... | collective-permute-start | bytes 5505032 | tf_op jit(solution)/shard_map/ppermute | solution.py:250
  114.4 1.3 %shard_map.61 = bf16[16,2,224,256]{3,2,1,0:T(8,128)(2,1)} custom-call(s32[1]{0:T(128)} %bitcast.core_ref, bf16[16,224,256]{2,1,0:T(8,128)(2,1)S(1)} %all_to_all.11.part_ref), custom_call_target="tpu_custom_call" | custom-call | bytes 3700000 | tf_op jit(solution)/shard_map/pallas_call | solution.py:220
  115.7 1.6 %collective-permute-done.16 = bf16[16,224,256]{2,1,0:T(8,128)(2,1)} collective-permute-done((bf16[16,224,256]{2,1,0:T(8,128)(2,1)S(1)}, bf16[16,224,256]{2,1,0:T(8,128)(2,1)}, u32[]{:S(2)}, u32[]{:S(2)}) %collective-permute-start.16) | collective-permute-done | bytes 1835040 | tf_op jit(solution)/shard_map/ppermute | solution.py:250
  117.3 2.8 %bitcast_dynamic-update-slice_fusion = bf16[16,2,224,256]{3,2,1,0:T(8,128)(2,1)} fusion(bf16[16,2,224,256]{3,2,1,0:T(8,128)(2,1)} %shard_map.61, s32[]{:T(128)S(6)} %select_n.22, bf16[16,224,256]{2,1,0:T(8,128)(2,1)} %collective-permute-done.16), kind=kLoop, calls=%fused_computation | loop fusion | bytes 3670020 | tf_op jit(solution)/shard_map/dynamic_update_slice | solution.py:300
  (38 shorter events, 10.3 us)
Async XLA Ops:
  0.6 0.8 copy-start
  1.5 0.9 copy-start.2
  9.7 1.6 %collective-permute-start = (f32[56,128]{1,0:T(8,128)S(1)}, f32[56,128]{1,0:T(8,128)S(1)}, u32[]{:S(2)}, u32[]{:S(2)}) collective-permute-start(f32[56,128]{1,0:T(8,128)S(1)} %get-tuple-element.9), channel_id=1, source_target_pairs={{0,8},{8,0},{1,9},{9,1},{2,10},{10,2},{3,11},{11,3},{4,12},{12,4},... | collective-permute-start | bytes 86024 | tf_op jit(solution)/shard_map/ppermute | solution.py:250
  11.3 29.7 %collective-permute-start.1 = (f32[16,224,256]{2,1,0:T(8,128)S(1)}, f32[16,224,256]{2,1,0:T(8,128)S(1)}, u32[]{:S(2)}, u32[]{:S(2)}) collective-permute-start(f32[16,224,256]{2,1,0:T(8,128)S(1)} %get-tuple-element.10), channel_id=1, source_target_pairs={{0,8},{8,0},{1,9},{9,1},{2,10},{10,2},{3,11},{11,3},{4,12},{12,4},... | collective-permute-start | bytes 11010056 | tf_op jit(solution)/shard_map/ppermute | solution.py:250
  11.7 3.6 %collective-permute-start.2 = (f32[56,128]{1,0:T(8,128)S(1)}, f32[56,128]{1,0:T(8,128)S(1)}, u32[]{:S(2)}, u32[]{:S(2)}) collective-permute-start(f32[56,128]{1,0:T(8,128)S(1)} %max.33), channel_id=1, source_target_pairs={{64,0},{128,64},{192,128},{0,192},{65,1},{129,65},{193,129},{1,193... | collective-permute-start | bytes 86024 | tf_op jit(solution)/shard_map/ppermute | solution.py:246
  14.2 4.2 %collective-permute-start.3 = (f32[56,128]{1,0:T(8,128)S(1)}, f32[56,128]{1,0:T(8,128)S(1)}, u32[]{:S(2)}, u32[]{:S(2)}) collective-permute-start(f32[56,128]{1,0:T(8,128)S(1)} %max.33), channel_id=1, source_target_pairs={{128,0},{192,64},{0,128},{64,192},{129,1},{193,65},{1,129},{65,193... | collective-permute-start | bytes 86024 | tf_op jit(solution)/shard_map/ppermute | solution.py:246
  14.7 4.0 %collective-permute-start.4 = (f32[56,128]{1,0:T(8,128)S(1)}, f32[56,128]{1,0:T(8,128)S(1)}, u32[]{:S(2)}, u32[]{:S(2)}) collective-permute-start(f32[56,128]{1,0:T(8,128)S(1)} %max.33), channel_id=1, source_target_pairs={{192,0},{0,64},{64,128},{128,192},{193,1},{1,65},{65,129},{129,193... | collective-permute-start | bytes 86024 | tf_op jit(solution)/shard_map/ppermute | solution.py:246
  18.7 3.9 %collective-permute-start.5 = (f32[56,128]{1,0:T(8,128)S(1)}, f32[56,128]{1,0:T(8,128)S(1)}, u32[]{:S(2)}, u32[]{:S(2)}) collective-permute-start(f32[56,128]{1,0:T(8,128)S(1)} %maximum_maximum_fusion.2), channel_id=1, source_target_pairs={{16,0},{32,16},{48,32},{0,48},{17,1},{33,17},{49,33},{1,49},{18,2}... | collective-permute-start | bytes 86024 | tf_op jit(solution)/shard_map/ppermute | solution.py:246
  21.5 4.2 %collective-permute-start.6 = (f32[56,128]{1,0:T(8,128)S(1)}, f32[56,128]{1,0:T(8,128)S(1)}, u32[]{:S(2)}, u32[]{:S(2)}) collective-permute-start(f32[56,128]{1,0:T(8,128)S(1)} %maximum_maximum_fusion.2), channel_id=1, source_target_pairs={{32,0},{48,16},{0,32},{16,48},{33,1},{49,17},{1,33},{17,49},{34,2}... | collective-permute-start | bytes 86024 | tf_op jit(solution)/shard_map/ppermute | solution.py:246
  21.9 4.2 %collective-permute-start.7 = (f32[56,128]{1,0:T(8,128)S(1)}, f32[56,128]{1,0:T(8,128)S(1)}, u32[]{:S(2)}, u32[]{:S(2)}) collective-permute-start(f32[56,128]{1,0:T(8,128)S(1)} %maximum_maximum_fusion.2), channel_id=1, source_target_pairs={{48,0},{0,16},{16,32},{32,48},{49,1},{1,17},{17,33},{33,49},{50,2}... | collective-permute-start | bytes 86024 | tf_op jit(solution)/shard_map/ppermute | solution.py:246
  26.1 3.0 %collective-permute-start.8 = (f32[56,128]{1,0:T(8,128)S(1)}, f32[56,128]{1,0:T(8,128)S(1)}, u32[]{:S(2)}, u32[]{:S(2)}) collective-permute-start(f32[56,128]{1,0:T(8,128)S(1)} %maximum_maximum_fusion.1), channel_id=1, source_target_pairs={{1,0},{2,1},{3,2},{4,3},{5,4},{6,5},{7,6},{0,7},{9,8},{10,9},{11,1... | collective-permute-start | bytes 86024 | tf_op jit(solution)/shard_map/ppermute | solution.py:246
  26.2 6.7 %collective-permute-start.9 = (f32[56,128]{1,0:T(8,128)S(1)}, f32[56,128]{1,0:T(8,128)S(1)}, u32[]{:S(2)}, u32[]{:S(2)}) collective-permute-start(f32[56,128]{1,0:T(8,128)S(1)} %maximum_maximum_fusion.1), channel_id=1, source_target_pairs={{7,0},{0,1},{1,2},{2,3},{3,4},{4,5},{5,6},{6,7},{15,8},{8,9},{9,10... | collective-permute-start | bytes 86024 | tf_op jit(solution)/shard_map/ppermute | solution.py:246
  32.9 6.1 %collective-permute-start.10 = (f32[56,128]{1,0:T(8,128)S(1)}, f32[56,128]{1,0:T(8,128)S(1)}, u32[]{:S(2)}, u32[]{:S(2)}) collective-permute-start(f32[56,128]{1,0:T(8,128)S(1)} %maximum_maximum_fusion), channel_id=1, source_target_pairs={{3,0},{4,1},{5,2},{6,3},{7,4},{0,5},{1,6},{2,7},{11,8},{12,9},{13,... | collective-permute-start | bytes 86024 | tf_op jit(solution)/shard_map/ppermute | solution.py:246
  35.2 5.8 %collective-permute-start.11 = (f32[56,128]{1,0:T(8,128)S(1)}, f32[56,128]{1,0:T(8,128)S(1)}, u32[]{:S(2)}, u32[]{:S(2)}) collective-permute-start(f32[56,128]{1,0:T(8,128)S(1)} %maximum_maximum_fusion), channel_id=1, source_target_pairs={{5,0},{6,1},{7,2},{0,3},{1,4},{2,5},{3,6},{4,7},{13,8},{14,9},{15,... | collective-permute-start | bytes 86024 | tf_op jit(solution)/shard_map/ppermute | solution.py:246
  43.8 32.9 %copy-start.1 = (s32[56,256]{1,0:T(8,128)S(1)}, s32[56,256]{1,0:T(8,128)}, u32[]{:S(2)}) copy-start(s32[56,256]{1,0:T(8,128)} %signs_hbm.1) | copy-start | bytes 172036
  43.9 39.4 %copy-start.3 = (f32[256,256]{1,0:T(8,128)S(1)}, f32[256,256]{1,0:T(8,128)}, u32[]{:S(2)}) copy-start(f32[256,256]{1,0:T(8,128)} %constant.60.clone) | copy-start | bytes 786436
  65.7 4.4 %collective-permute-start.12 = (bf16[224,256]{1,0:T(8,128)(2,1)S(1)}, bf16[224,256]{1,0:T(8,128)(2,1)S(1)}, u32[]{:S(2)}, u32[]{:S(2)}) collective-permute-start(bf16[224,256]{1,0:T(8,128)(2,1)S(1)} %reduce_sum.12), channel_id=1, source_target_pairs={{0,1},{1,0},{2,3},{3,2},{4,5},{5,4},{6,7},{7,6},{8,9},{9,8},{10,11... | collective-permute-start | bytes 344072 | tf_op jit(solution)/shard_map/ppermute | solution.py:250
  67.7 5.8 %collective-permute-start.13 = (bf16[224,256]{1,0:T(8,128)(2,1)S(1)}, bf16[224,256]{1,0:T(8,128)(2,1)S(1)}, u32[]{:S(2)}, u32[]{:S(2)}) collective-permute-start(bf16[224,256]{1,0:T(8,128)(2,1)S(1)} %reduce_sum.12), channel_id=1, source_target_pairs={{0,2},{1,3},{2,0},{3,1},{4,6},{5,7},{6,4},{7,5},{8,10},{9,11},{10,... | collective-permute-start | bytes 344072 | tf_op jit(solution)/shard_map/ppermute | solution.py:250
  69.5 5.9 %collective-permute-start.14 = (bf16[224,256]{1,0:T(8,128)(2,1)S(1)}, bf16[224,256]{1,0:T(8,128)(2,1)S(1)}, u32[]{:S(2)}, u32[]{:S(2)}) collective-permute-start(bf16[224,256]{1,0:T(8,128)(2,1)S(1)} %reduce_sum.12), channel_id=1, source_target_pairs={{0,3},{1,2},{2,1},{3,0},{4,7},{5,6},{6,5},{7,4},{8,11},{9,10},{10,... | collective-permute-start | bytes 344072 | tf_op jit(solution)/shard_map/ppermute | solution.py:250
  75.4 7.8 %collective-permute-start.15 = (bf16[224,256]{1,0:T(8,128)(2,1)S(1)}, bf16[224,256]{1,0:T(8,128)(2,1)S(1)}, u32[]{:S(2)}, u32[]{:S(2)}) collective-permute-start(bf16[224,256]{1,0:T(8,128)(2,1)S(1)} %add_convert_fusion), channel_id=1, source_target_pairs={{0,7},{1,6},{2,5},{3,4},{4,3},{5,2},{6,1},{7,0},{8,15},{9,14},{10,... | collective-permute-start | bytes 344072 | tf_op jit(solution)/shard_map/ppermute | solution.py:254
  103.6 13.7 %collective-permute-start.16 = (bf16[16,224,256]{2,1,0:T(8,128)(2,1)S(1)}, bf16[16,224,256]{2,1,0:T(8,128)(2,1)}, u32[]{:S(2)}, u32[]{:S(2)}) collective-permute-start(bf16[16,224,256]{2,1,0:T(8,128)(2,1)S(1)} %all_to_all.11.part_ref), channel_id=1, source_target_pairs={{0,8},{8,0},{1,9},{9,1},{2,10},{10,2},{3,11},{11,3},{4,12},{12,4},... | collective-permute-start | bytes 5505032 | tf_op jit(solution)/shard_map/ppermute | solution.py:250

commit v3 on v2

--- a/solution.py
+++ b/solution.py
@@ -188,7 +188,7 @@
                 sum_ref[j, :, lane : lane + COLS] = (mine + other).astype(jnp.bfloat16)
         return carry
 
-    lax.fori_loop(0, STEPS, step, 0)
+    lax.fori_loop(0, STEPS, step, 0, unroll=True)
 
 
 def quantize(core, keep, other, scale):

time: 120 us -> 120 us (level)
  no operation moved by 1% of the time
where the time goes in v3:
time: 120 us
  blocking collectives  41.3 us (34%)
  starting transfers between devices  30.2 us (25%)
  waiting for transfers between devices  29.8 us (25%)
  Pallas kernels  11 us (9%)
  local copies, waits for them, and re-layouts  5.43 us (5%)
    all_to_all x1, blocking collectives, body(): parts = lax.all_to_all(parts, ('x', 'y'), 0, 0, tiled=True)  21.5 us
    all_to_all x1, blocking collectives, body(): grad = lax.all_to_all(grad, ('x', 'y'), 0, 0, tiled=True)  19.7 us
    ppermute x10, waiting for transfers between devices, shift(): lax.ppermute(value, axis, [((i + step) % size, i) for i in range(size)])  15.4 us
    ppermute x6, starting transfers between devices, flip(): return lax.ppermute(value, axis, [(i, i ^ bit) for i in range(size)])  15.1 us
    ppermute x10, starting transfers between devices, shift(): lax.ppermute(value, axis, [((i + step) % size, i) for i in range(size)])  13.8 us
    ppermute x6, waiting for transfers between devices, flip(): return lax.ppermute(value, axis, [(i, i ^ bit) for i in range(size)])  8.27 us
    pallas_call x1, Pallas kernels, rotate(): pl.pallas_call(rotate_kernel, in_specs=[IN_SMEM, IN_ANY, IN_ANY, IN_ANY],...  7.36 us
    ppermute x1, waiting for transfers between devices, mirror(): return lax.ppermute(value, axis, [(i, size - 1 - i) for i in range(size)])  6.07 us
  transfers between devices with their start and end apart: 17, of which 14 were waited for; matrix products, arithmetic and copies ran while one was open for 1% of the time, Pallas kernels for 1%

profile of v3, /device:TPU:33, one launch (start us, length us, event | category | flops | bytes accessed | tf_op | source)
XLA Modules:
  0.0 119.6 jit_solution(13864290872269134730)
XLA Ops:
  2.3 7.4 %shard_map.59 = (f32[16,224,256]{2,1,0:T(8,128)S(1)}, f32[16,224,256]{2,1,0:T(8,128)S(1)}, f32[56,128]{1,0:T(8,128)S(1)}) custom-call(s32[1]{0:T(128)} %bitcast.core_ref, bf16[320,14336]{1,0:T(8,128)(2,1)} %acts_hbm.1, bf16[320,128]{1,0:T(8,128)(2,1)S(1)} %copy-done.2, s32[56,256]{1,0:T(8,128)S(1)} %copy-done), custom_call_target="tpu_custom_call" | custom-call | flops 3053453312 | bytes 17000000 | tf_op jit(solution)/shard_map/pallas_call | solution.py:150
  11.7 2.5 %collective-permute-start.2 = (f32[56,128]{1,0:T(8,128)S(1)}, f32[56,128]{1,0:T(8,128)S(1)}, u32[]{:S(2)}, u32[]{:S(2)}) collective-permute-start(f32[56,128]{1,0:T(8,128)S(1)} %max.33), channel_id=1, source_target_pairs={{64,0},{128,64},{192,128},{0,192},{65,1},{129,65},{193,129},{1,193... | collective-permute-start | bytes 86024 | tf_op jit(solution)/shard_map/ppermute | solution.py:246
  15.3 3.1 %collective-permute-done.3 = f32[56,128]{1,0:T(8,128)S(1)} collective-permute-done((f32[56,128]{1,0:T(8,128)S(1)}, f32[56,128]{1,0:T(8,128)S(1)}, u32[]{:S(2)}, u32[]{:S(2)}) %collective-permute-start.3) | collective-permute-done | bytes 28704 | tf_op jit(solution)/shard_map/ppermute | solution.py:246
  18.7 2.8 %collective-permute-start.5 = (f32[56,128]{1,0:T(8,128)S(1)}, f32[56,128]{1,0:T(8,128)S(1)}, u32[]{:S(2)}, u32[]{:S(2)}) collective-permute-start(f32[56,128]{1,0:T(8,128)S(1)} %maximum_maximum_fusion.2), channel_id=1, source_target_pairs={{16,0},{32,16},{48,32},{0,48},{17,1},{33,17},{49,33},{1,49},{18,2}... | collective-permute-start | bytes 86024 | tf_op jit(solution)/shard_map/ppermute | solution.py:246
  22.6 3.2 %collective-permute-done.6 = f32[56,128]{1,0:T(8,128)S(1)} collective-permute-done((f32[56,128]{1,0:T(8,128)S(1)}, f32[56,128]{1,0:T(8,128)S(1)}, u32[]{:S(2)}, u32[]{:S(2)}) %collective-permute-start.6) | collective-permute-done | bytes 28704 | tf_op jit(solution)/shard_map/ppermute | solution.py:246
  26.2 1.7 %collective-permute-start.9 = (f32[56,128]{1,0:T(8,128)S(1)}, f32[56,128]{1,0:T(8,128)S(1)}, u32[]{:S(2)}, u32[]{:S(2)}) collective-permute-start(f32[56,128]{1,0:T(8,128)S(1)} %maximum_maximum_fusion.1), channel_id=1, source_target_pairs={{7,0},{0,1},{1,2},{2,3},{3,4},{4,5},{5,6},{6,7},{15,8},{8,9},{9,10... | collective-permute-start | bytes 86024 | tf_op jit(solution)/shard_map/ppermute | solution.py:246
  29.1 3.8 %collective-permute-done.9 = f32[56,128]{1,0:T(8,128)S(1)} collective-permute-done((f32[56,128]{1,0:T(8,128)S(1)}, f32[56,128]{1,0:T(8,128)S(1)}, u32[]{:S(2)}, u32[]{:S(2)}) %collective-permute-start.9) | collective-permute-done | bytes 28704 | tf_op jit(solution)/shard_map/ppermute | solution.py:246
  32.9 2.4 %collective-permute-start.10 = (f32[56,128]{1,0:T(8,128)S(1)}, f32[56,128]{1,0:T(8,128)S(1)}, u32[]{:S(2)}, u32[]{:S(2)}) collective-permute-start(f32[56,128]{1,0:T(8,128)S(1)} %maximum_maximum_fusion), channel_id=1, source_target_pairs={{3,0},{4,1},{5,2},{6,3},{7,4},{0,5},{1,6},{2,7},{11,8},{12,9},{13,... | collective-permute-start | bytes 86024 | tf_op jit(solution)/shard_map/ppermute | solution.py:246
  35.2 2.2 %collective-permute-start.11 = (f32[56,128]{1,0:T(8,128)S(1)}, f32[56,128]{1,0:T(8,128)S(1)}, u32[]{:S(2)}, u32[]{:S(2)}) collective-permute-start(f32[56,128]{1,0:T(8,128)S(1)} %maximum_maximum_fusion), channel_id=1, source_target_pairs={{5,0},{6,1},{7,2},{0,3},{1,4},{2,5},{3,6},{4,7},{13,8},{14,9},{15,... | collective-permute-start | bytes 86024 | tf_op jit(solution)/shard_map/ppermute | solution.py:246
  37.4 1.6 %collective-permute-done.10 = f32[56,128]{1,0:T(8,128)S(1)} collective-permute-done((f32[56,128]{1,0:T(8,128)S(1)}, f32[56,128]{1,0:T(8,128)S(1)}, u32[]{:S(2)}, u32[]{:S(2)}) %collective-permute-start.10) | collective-permute-done | bytes 28704 | tf_op jit(solution)/shard_map/ppermute | solution.py:246
  39.0 2.0 %collective-permute-done.11 = f32[56,128]{1,0:T(8,128)S(1)} collective-permute-done((f32[56,128]{1,0:T(8,128)S(1)}, f32[56,128]{1,0:T(8,128)S(1)}, u32[]{:S(2)}, u32[]{:S(2)}) %collective-permute-start.11) | collective-permute-done | bytes 28704 | tf_op jit(solution)/shard_map/ppermute | solution.py:246
  41.0 2.3 %shard_map.60 = bf16[16,224,256]{2,1,0:T(8,128)(2,1)S(1)} custom-call(s32[1]{0:T(128)} %bitcast.core_ref, f32[16,224,256]{2,1,0:T(8,128)S(1)} %get-tuple-element.7.keep_ref, f32[16,224,256]{2,1,0:T(8,128)S(1)} %collective-permute-done.1.other_ref, f32[56,128]{1,0:T(8,128)S(1)} %maximum_add_fusion.scale_ref), custom_call_target="tpu_custom_call" | custom-call | flops 7340032 | bytes 9200000 | tf_op jit(solution)/shard_map/pallas_call | solution.py:195
  43.3 21.5 %all_to_all.10 = bf16[16,224,256]{2,1,0:T(8,128)(2,1)S(1)} all-to-all(bf16[16,224,256]{2,1,0:T(8,128)(2,1)S(1)} %shard_map.60), channel_id=1, replica_groups=mesh['x'=4,'y'=4,'c'=2,'z'=8] {'x','y'}, dimensions={0} | all-to-all | bytes 3670016 | tf_op jit(solution)/shard_map/all_to_all | solution.py:288
  65.1 2.0 %collective-permute-start.12 = (bf16[224,256]{1,0:T(8,128)(2,1)S(1)}, bf16[224,256]{1,0:T(8,128)(2,1)S(1)}, u32[]{:S(2)}, u32[]{:S(2)}) collective-permute-start(bf16[224,256]{1,0:T(8,128)(2,1)S(1)} %reduce_sum.12), channel_id=1, source_target_pairs={{0,1},{1,0},{2,3},{3,2},{4,5},{5,4},{6,7},{7,6},{8,9},{9,8},{10,11... | collective-permute-start | bytes 344072 | tf_op jit(solution)/shard_map/ppermute | solution.py:250
  67.2 1.8 %collective-permute-start.13 = (bf16[224,256]{1,0:T(8,128)(2,1)S(1)}, bf16[224,256]{1,0:T(8,128)(2,1)S(1)}, u32[]{:S(2)}, u32[]{:S(2)}) collective-permute-start(bf16[224,256]{1,0:T(8,128)(2,1)S(1)} %reduce_sum.12), channel_id=1, source_target_pairs={{0,2},{1,3},{2,0},{3,1},{4,6},{5,7},{6,4},{7,5},{8,10},{9,11},{10,... | collective-permute-start | bytes 344072 | tf_op jit(solution)/shard_map/ppermute | solution.py:250
  69.7 3.3 %collective-permute-done.13 = bf16[224,256]{1,0:T(8,128)(2,1)S(1)} collective-permute-done((bf16[224,256]{1,0:T(8,128)(2,1)S(1)}, bf16[224,256]{1,0:T(8,128)(2,1)S(1)}, u32[]{:S(2)}, u32[]{:S(2)}) %collective-permute-start.13) | collective-permute-done | bytes 114720 | tf_op jit(solution)/shard_map/ppermute | solution.py:250
  72.9 1.9 %collective-permute-done.14 = bf16[224,256]{1,0:T(8,128)(2,1)S(1)} collective-permute-done((bf16[224,256]{1,0:T(8,128)(2,1)S(1)}, bf16[224,256]{1,0:T(8,128)(2,1)S(1)}, u32[]{:S(2)}, u32[]{:S(2)}) %collective-permute-start.14) | collective-permute-done | bytes 114720 | tf_op jit(solution)/shard_map/ppermute | solution.py:250
  74.9 1.3 %collective-permute-start.15 = (bf16[224,256]{1,0:T(8,128)(2,1)S(1)}, bf16[224,256]{1,0:T(8,128)(2,1)S(1)}, u32[]{:S(2)}, u32[]{:S(2)}) collective-permute-start(bf16[224,256]{1,0:T(8,128)(2,1)S(1)} %add_convert_fusion), channel_id=1, source_target_pairs={{0,7},{1,6},{2,5},{3,4},{4,3},{5,2},{6,1},{7,0},{8,15},{9,14},{10,... | collective-permute-start | bytes 344072 | tf_op jit(solution)/shard_map/ppermute | solution.py:254
  76.6 6.1 %collective-permute-done.15 = bf16[224,256]{1,0:T(8,128)(2,1)S(1)} collective-permute-done((bf16[224,256]{1,0:T(8,128)(2,1)S(1)}, bf16[224,256]{1,0:T(8,128)(2,1)S(1)}, u32[]{:S(2)}, u32[]{:S(2)}) %collective-permute-start.15) | collective-permute-done | bytes 114720 | tf_op jit(solution)/shard_map/ppermute | solution.py:254
  83.3 19.7 %all_to_all.11.part_ref = bf16[16,224,256]{2,1,0:T(8,128)(2,1)S(1)} all-to-all(bf16[16,224,256]{2,1,0:T(8,128)(2,1)S(1)} %broadcast_in_dim.7), channel_id=1, replica_groups=mesh['x'=4,'y'=4,'c'=2,'z'=8] {'x','y'}, dimensions={0} | all-to-all | bytes 3670016 | tf_op jit(solution)/shard_map/all_to_all | solution.py:297
  103.0 10.2 %collective-permute-start.16 = (bf16[16,224,256]{2,1,0:T(8,128)(2,1)S(1)}, bf16[16,224,256]{2,1,0:T(8,128)(2,1)}, u32[]{:S(2)}, u32[]{:S(2)}) collective-permute-start(bf16[16,224,256]{2,1,0:T(8,128)(2,1)S(1)} %all_to_all.11.part_ref), channel_id=1, source_target_pairs={{0,8},{8,0},{1,9},{9,1},{2,10},{10,2},{3,11},{11,3},{4,12},{12,4},... | collective-permute-start | bytes 5505032 | tf_op jit(solution)/shard_map/ppermute | solution.py:250
  113.8 1.3 %shard_map.61 = bf16[16,2,224,256]{3,2,1,0:T(8,128)(2,1)} custom-call(s32[1]{0:T(128)} %bitcast.core_ref, bf16[16,224,256]{2,1,0:T(8,128)(2,1)S(1)} %all_to_all.11.part_ref), custom_call_target="tpu_custom_call" | custom-call | bytes 3700000 | tf_op jit(solution)/shard_map/pallas_call | solution.py:220
  115.2 1.6 %collective-permute-done.16 = bf16[16,224,256]{2,1,0:T(8,128)(2,1)} collective-permute-done((bf16[16,224,256]{2,1,0:T(8,128)(2,1)S(1)}, bf16[16,224,256]{2,1,0:T(8,128)(2,1)}, u32[]{:S(2)}, u32[]{:S(2)}) %collective-permute-start.16) | collective-permute-done | bytes 1835040 | tf_op jit(solution)/shard_map/ppermute | solution.py:250
  116.8 2.8 %bitcast_dynamic-update-slice_fusion = bf16[16,2,224,256]{3,2,1,0:T(8,128)(2,1)} fusion(bf16[16,2,224,256]{3,2,1,0:T(8,128)(2,1)} %shard_map.61, s32[]{:T(128)S(6)} %select_n.22, bf16[16,224,256]{2,1,0:T(8,128)(2,1)} %collective-permute-done.16), kind=kLoop, calls=%fused_computation | loop fusion | bytes 3670020 | tf_op jit(solution)/shard_map/dynamic_update_slice | solution.py:300
  (38 shorter events, 10.4 us)
Async XLA Ops:
  0.6 0.8 copy-start
  1.5 0.9 copy-start.2
  9.7 1.6 %collective-permute-start = (f32[56,128]{1,0:T(8,128)S(1)}, f32[56,128]{1,0:T(8,128)S(1)}, u32[]{:S(2)}, u32[]{:S(2)}) collective-permute-start(f32[56,128]{1,0:T(8,128)S(1)} %get-tuple-element.9), channel_id=1, source_target_pairs={{0,8},{8,0},{1,9},{9,1},{2,10},{10,2},{3,11},{11,3},{4,12},{12,4},... | collective-permute-start | bytes 86024 | tf_op jit(solution)/shard_map/ppermute | solution.py:250
  11.3 29.7 %collective-permute-start.1 = (f32[16,224,256]{2,1,0:T(8,128)S(1)}, f32[16,224,256]{2,1,0:T(8,128)S(1)}, u32[]{:S(2)}, u32[]{:S(2)}) collective-permute-start(f32[16,224,256]{2,1,0:T(8,128)S(1)} %get-tuple-element.10), channel_id=1, source_target_pairs={{0,8},{8,0},{1,9},{9,1},{2,10},{10,2},{3,11},{11,3},{4,12},{12,4},... | collective-permute-start | bytes 11010056 | tf_op jit(solution)/shard_map/ppermute | solution.py:250
  11.7 3.6 %collective-permute-start.2 = (f32[56,128]{1,0:T(8,128)S(1)}, f32[56,128]{1,0:T(8,128)S(1)}, u32[]{:S(2)}, u32[]{:S(2)}) collective-permute-start(f32[56,128]{1,0:T(8,128)S(1)} %max.33), channel_id=1, source_target_pairs={{64,0},{128,64},{192,128},{0,192},{65,1},{129,65},{193,129},{1,193... | collective-permute-start | bytes 86024 | tf_op jit(solution)/shard_map/ppermute | solution.py:246
  14.2 4.2 %collective-permute-start.3 = (f32[56,128]{1,0:T(8,128)S(1)}, f32[56,128]{1,0:T(8,128)S(1)}, u32[]{:S(2)}, u32[]{:S(2)}) collective-permute-start(f32[56,128]{1,0:T(8,128)S(1)} %max.33), channel_id=1, source_target_pairs={{128,0},{192,64},{0,128},{64,192},{129,1},{193,65},{1,129},{65,193... | collective-permute-start | bytes 86024 | tf_op jit(solution)/shard_map/ppermute | solution.py:246
  14.7 4.0 %collective-permute-start.4 = (f32[56,128]{1,0:T(8,128)S(1)}, f32[56,128]{1,0:T(8,128)S(1)}, u32[]{:S(2)}, u32[]{:S(2)}) collective-permute-start(f32[56,128]{1,0:T(8,128)S(1)} %max.33), channel_id=1, source_target_pairs={{192,0},{0,64},{64,128},{128,192},{193,1},{1,65},{65,129},{129,193... | collective-permute-start | bytes 86024 | tf_op jit(solution)/shard_map/ppermute | solution.py:246
  18.7 3.9 %collective-permute-start.5 = (f32[56,128]{1,0:T(8,128)S(1)}, f32[56,128]{1,0:T(8,128)S(1)}, u32[]{:S(2)}, u32[]{:S(2)}) collective-permute-start(f32[56,128]{1,0:T(8,128)S(1)} %maximum_maximum_fusion.2), channel_id=1, source_target_pairs={{16,0},{32,16},{48,32},{0,48},{17,1},{33,17},{49,33},{1,49},{18,2}... | collective-permute-start | bytes 86024 | tf_op jit(solution)/shard_map/ppermute | solution.py:246
  21.5 4.2 %collective-permute-start.6 = (f32[56,128]{1,0:T(8,128)S(1)}, f32[56,128]{1,0:T(8,128)S(1)}, u32[]{:S(2)}, u32[]{:S(2)}) collective-permute-start(f32[56,128]{1,0:T(8,128)S(1)} %maximum_maximum_fusion.2), channel_id=1, source_target_pairs={{32,0},{48,16},{0,32},{16,48},{33,1},{49,17},{1,33},{17,49},{34,2}... | collective-permute-start | bytes 86024 | tf_op jit(solution)/shard_map/ppermute | solution.py:246
  21.9 4.2 %collective-permute-start.7 = (f32[56,128]{1,0:T(8,128)S(1)}, f32[56,128]{1,0:T(8,128)S(1)}, u32[]{:S(2)}, u32[]{:S(2)}) collective-permute-start(f32[56,128]{1,0:T(8,128)S(1)} %maximum_maximum_fusion.2), channel_id=1, source_target_pairs={{48,0},{0,16},{16,32},{32,48},{49,1},{1,17},{17,33},{33,49},{50,2}... | collective-permute-start | bytes 86024 | tf_op jit(solution)/shard_map/ppermute | solution.py:246
  26.1 3.0 %collective-permute-start.8 = (f32[56,128]{1,0:T(8,128)S(1)}, f32[56,128]{1,0:T(8,128)S(1)}, u32[]{:S(2)}, u32[]{:S(2)}) collective-permute-start(f32[56,128]{1,0:T(8,128)S(1)} %maximum_maximum_fusion.1), channel_id=1, source_target_pairs={{1,0},{2,1},{3,2},{4,3},{5,4},{6,5},{7,6},{0,7},{9,8},{10,9},{11,1... | collective-permute-start | bytes 86024 | tf_op jit(solution)/shard_map/ppermute | solution.py:246
  26.2 6.7 %collective-permute-start.9 = (f32[56,128]{1,0:T(8,128)S(1)}, f32[56,128]{1,0:T(8,128)S(1)}, u32[]{:S(2)}, u32[]{:S(2)}) collective-permute-start(f32[56,128]{1,0:T(8,128)S(1)} %maximum_maximum_fusion.1), channel_id=1, source_target_pairs={{7,0},{0,1},{1,2},{2,3},{3,4},{4,5},{5,6},{6,7},{15,8},{8,9},{9,10... | collective-permute-start | bytes 86024 | tf_op jit(solution)/shard_map/ppermute | solution.py:246
  32.9 6.1 %collective-permute-start.10 = (f32[56,128]{1,0:T(8,128)S(1)}, f32[56,128]{1,0:T(8,128)S(1)}, u32[]{:S(2)}, u32[]{:S(2)}) collective-permute-start(f32[56,128]{1,0:T(8,128)S(1)} %maximum_maximum_fusion), channel_id=1, source_target_pairs={{3,0},{4,1},{5,2},{6,3},{7,4},{0,5},{1,6},{2,7},{11,8},{12,9},{13,... | collective-permute-start | bytes 86024 | tf_op jit(solution)/shard_map/ppermute | solution.py:246
  35.2 5.8 %collective-permute-start.11 = (f32[56,128]{1,0:T(8,128)S(1)}, f32[56,128]{1,0:T(8,128)S(1)}, u32[]{:S(2)}, u32[]{:S(2)}) collective-permute-start(f32[56,128]{1,0:T(8,128)S(1)} %maximum_maximum_fusion), channel_id=1, source_target_pairs={{5,0},{6,1},{7,2},{0,3},{1,4},{2,5},{3,6},{4,7},{13,8},{14,9},{15,... | collective-permute-start | bytes 86024 | tf_op jit(solution)/shard_map/ppermute | solution.py:246
  43.3 32.9 %copy-start.1 = (s32[56,256]{1,0:T(8,128)S(1)}, s32[56,256]{1,0:T(8,128)}, u32[]{:S(2)}) copy-start(s32[56,256]{1,0:T(8,128)} %signs_hbm.1) | copy-start | bytes 172036
  43.3 39.4 %copy-start.3 = (f32[256,256]{1,0:T(8,128)S(1)}, f32[256,256]{1,0:T(8,128)}, u32[]{:S(2)}) copy-start(f32[256,256]{1,0:T(8,128)} %constant.60.clone) | copy-start | bytes 786436
  65.1 4.5 %collective-permute-start.12 = (bf16[224,256]{1,0:T(8,128)(2,1)S(1)}, bf16[224,256]{1,0:T(8,128)(2,1)S(1)}, u32[]{:S(2)}, u32[]{:S(2)}) collective-permute-start(bf16[224,256]{1,0:T(8,128)(2,1)S(1)} %reduce_sum.12), channel_id=1, source_target_pairs={{0,1},{1,0},{2,3},{3,2},{4,5},{5,4},{6,7},{7,6},{8,9},{9,8},{10,11... | collective-permute-start | bytes 344072 | tf_op jit(solution)/shard_map/ppermute | solution.py:250
  67.2 5.8 %collective-permute-start.13 = (bf16[224,256]{1,0:T(8,128)(2,1)S(1)}, bf16[224,256]{1,0:T(8,128)(2,1)S(1)}, u32[]{:S(2)}, u32[]{:S(2)}) collective-permute-start(bf16[224,256]{1,0:T(8,128)(2,1)S(1)} %reduce_sum.12), channel_id=1, source_target_pairs={{0,2},{1,3},{2,0},{3,1},{4,6},{5,7},{6,4},{7,5},{8,10},{9,11},{10,... | collective-permute-start | bytes 344072 | tf_op jit(solution)/shard_map/ppermute | solution.py:250
  68.9 5.9 %collective-permute-start.14 = (bf16[224,256]{1,0:T(8,128)(2,1)S(1)}, bf16[224,256]{1,0:T(8,128)(2,1)S(1)}, u32[]{:S(2)}, u32[]{:S(2)}) collective-permute-start(bf16[224,256]{1,0:T(8,128)(2,1)S(1)} %reduce_sum.12), channel_id=1, source_target_pairs={{0,3},{1,2},{2,1},{3,0},{4,7},{5,6},{6,5},{7,4},{8,11},{9,10},{10,... | collective-permute-start | bytes 344072 | tf_op jit(solution)/shard_map/ppermute | solution.py:250
  74.9 7.8 %collective-permute-start.15 = (bf16[224,256]{1,0:T(8,128)(2,1)S(1)}, bf16[224,256]{1,0:T(8,128)(2,1)S(1)}, u32[]{:S(2)}, u32[]{:S(2)}) collective-permute-start(bf16[224,256]{1,0:T(8,128)(2,1)S(1)} %add_convert_fusion), channel_id=1, source_target_pairs={{0,7},{1,6},{2,5},{3,4},{4,3},{5,2},{6,1},{7,0},{8,15},{9,14},{10,... | collective-permute-start | bytes 344072 | tf_op jit(solution)/shard_map/ppermute | solution.py:254
  103.0 13.7 %collective-permute-start.16 = (bf16[16,224,256]{2,1,0:T(8,128)(2,1)S(1)}, bf16[16,224,256]{2,1,0:T(8,128)(2,1)}, u32[]{:S(2)}, u32[]{:S(2)}) collective-permute-start(bf16[16,224,256]{2,1,0:T(8,128)(2,1)S(1)} %all_to_all.11.part_ref), channel_id=1, source_target_pairs={{0,8},{8,0},{1,9},{9,1},{2,10},{10,2},{3,11},{11,3},{4,12},{12,4},... | collective-permute-start | bytes 5505032 | tf_op jit(solution)/shard_map/ppermute | solution.py:250
